TPU v7x, 32 devices: a whole 2x2x4 slice. The times are simulated.
32 devices in a mesh: dp: 8 (over z, y), rep: 4 (over x, core).
Axes of the slice: x: 2, y: 2, z: 4, core: 2. Of those that a mesh axis runs over, the one named last changes fastest.
Arguments:
- clip_input: bfloat16 [32, 4, 20, 20, 832], P(('dp', 'rep')), may hold values from -6 to 6
- cotangent: bfloat16 [32, 2, 10, 10, 832], P(('dp', 'rep')), may hold values from -6 to 6
- clip_group: int32 [32], P(('dp', 'rep')), may hold values from 0 to 2
- crop_sides: int32 [3], replicated, may hold values from 14 to 20, as said below
- w_single: bfloat16 [2, 832, 256], replicated, may hold values from -0.21875 to 0.21875
- w_reduce: bfloat16 [2, 832, 160], replicated, may hold values from -0.21875 to 0.21875
- w_spatial: bfloat16 [2, 3, 3, 3, 160, 320], replicated, may hold values from -0.09375 to 0.09375
- w_squeeze: bfloat16 [2, 832, 32], replicated, may hold values from -0.21875 to 0.21875
- w_narrow: bfloat16 [2, 3, 3, 3, 32, 128], replicated, may hold values from -0.21875 to 0.21875
- w_project: bfloat16 [2, 832, 128], replicated, may hold values from -0.21875 to 0.21875
- bn_scale: float32 [2, 1024], replicated, may hold values from 0.1 to 1.9
- bn_shift: float32 [2, 1024], replicated, may hold values from -3 to 3
Outputs:
- activations: bfloat16 [32, 2, 10, 10, 832], P(('dp', 'rep'))
- input_grad: bfloat16 [32, 4, 20, 20, 832], P(('dp', 'rep'))
- grad_single: float32 [2, 832, 256], replicated
- grad_reduce: float32 [2, 832, 160], replicated
- grad_spatial: float32 [2, 3, 3, 3, 160, 320], replicated
- grad_squeeze: float32 [2, 832, 32], replicated
- grad_narrow: float32 [2, 3, 3, 3, 32, 128], replicated
- grad_project: float32 [2, 832, 128], replicated
- grad_scale: float32 [2, 1024], replicated
- grad_shift: float32 [2, 1024], replicated
Inputs may be any that keep to these rules, and one draw needn't show every extreme that they name: `crop_sides`: the three entries are 20, 16 and 14, in an order drawn from the seed.
All inputs are finite; a program needn't handle non-finite values.
Results may differ from a plain program's by a relative error of at most 0.015.
Values sent between devices are 32-bit elements; how exact they have to be, the bound alone decides.
No kernel may reach another device: no remote copies, remote signals or barrier semaphores. Data moves between devices by JAX's collectives and lax.ppermute only.
A program may use at most 320 MiB of HBM per device.

v0:
```python
import functools

import jax
import jax.numpy as jnp
from jax import lax
from jax.experimental import pallas as pl
from jax.experimental.pallas import tpu as pltpu
from jax.sharding import PartitionSpec as P

AXES = ("dp", "rep")
F32 = jnp.float32
LOW = jnp.bfloat16
EDGE = 32
TAPS = [(dh, dw) for dh in (-1, 0, 1) for dw in (-1, 0, 1)]
UNIT_TILES = [("b", 0), ("b", 1), ("c", 0), ("c", 1), ("c", 2), ("c", 3), ("b", 2)]
VMEM = pl.BlockSpec(memory_space=pltpu.VMEM)
SMEM = pl.BlockSpec(memory_space=pltpu.SMEM)
MIB = 1024 * 1024


def struct(shape, kind):
    return jax.ShapeDtypeStruct(shape, kind)


def scoped(scratch, room):
    total = 0
    for item in scratch:
        if isinstance(item, jax.core.ShapedArray) or hasattr(item, "shape"):
            shape = item.shape
            if len(shape) >= 2:
                size = -(-shape[-1] // 128) * 128 * -(-shape[-2] // 8) * 8 * jnp.dtype(item.dtype).itemsize
                for n in shape[:-2]:
                    size *= n
                total += size
    return total + room * MIB


def call(body, ins, outs, scratch=(), scalars=2, room=8, flops=0, name=None):
    return pl.pallas_call(
        body,
        out_shape=tuple(outs),
        in_specs=[SMEM] * scalars + [VMEM] * (len(ins) - scalars),
        out_specs=tuple([VMEM] * len(outs)),
        scratch_shapes=list(scratch),
        compiler_params=pltpu.CompilerParams(vmem_limit_bytes=scoped(scratch, room)),
        cost_estimate=pl.CostEstimate(
            flops=flops,
            bytes_accessed=sum(x.size * x.dtype.itemsize for x in ins),
            transcendentals=0,
        ),
        name=name,
    )(*ins)


def tile(index, width=1):
    return slice(index * 128, (index + width) * 128)


def lanes():
    return lax.broadcasted_iota(jnp.int32, (1, 128), 1)


def sigmoid(v):
    return 0.5 * jnp.tanh(0.5 * v) + 0.5


def places(frame, side):
    at = lax.broadcasted_iota(jnp.int32, (frame, 1), 0).astype(F32)
    row = jnp.floor((at + 0.5) * (1.0 / side))
    return row, at - row * side


def crop_mask(frame, side, crop):
    row, column = places(frame, side)
    return jnp.where((row < crop) & (column < crop), 1.0, 0.0).astype(F32)


def column_mask(frame, side, step):
    row, column = places(frame, side)
    inside = (column + step > -0.5) & (column + step < side - 0.5)
    return jnp.where(inside, 1.0, 0.0).astype(F32)


def crop_of(group_ref, sides_ref, halved):
    crop = sides_ref[group_ref[0]]
    if halved:
        crop = lax.shift_right_logical(crop, 1)
    return crop.astype(F32)


def moments(sums, count):
    mean = sums[0:1] / count
    square = sums[1:2] / count
    return mean, lax.rsqrt(square - mean * mean + 1e-05)


def back_terms(sums, count, gamma, inverse):
    scale = gamma * inverse
    return scale, scale * (sums[0:1] / count), scale * (sums[1:2] / count)


def add_sums(ref, at, first, second):
    ref[0:1, at] += jnp.sum(first, axis=0, keepdims=True)
    ref[1:2, at] += jnp.sum(second, axis=0, keepdims=True)


def neighbour_sum(values, around, frame, side, put):
    frames = len(values)
    left = column_mask(frame, side, -1)
    right = column_mask(frame, side, 1)
    for t in range(frames):
        total = values[t]
        if t > 0:
            total = total + values[t - 1]
        if t < frames - 1:
            total = total + values[t + 1]
        around[EDGE : EDGE + frame, tile(0)] = total
        total = (
            total
            + around[EDGE - side : EDGE - side + frame, tile(0)]
            + around[EDGE + side : EDGE + side + frame, tile(0)]
        )
        around[EDGE : EDGE + frame, tile(0)] = total
        total = (
            total
            + around[EDGE - 1 : EDGE - 1 + frame, tile(0)] * left
            + around[EDGE + 1 : EDGE + 1 + frame, tile(0)] * right
        )
        put(t, total * (1.0 / 27.0))


def clear_edges(around, frame):
    width = around.shape[1]
    around[0:EDGE, :] = jnp.zeros((EDGE, width), F32)
    around[EDGE + frame : 2 * EDGE + frame, :] = jnp.zeros((EDGE, width), F32)


def dot(a, b):
    return lax.dot_general(a, b, (((1,), (0,)), ((), ())), preferred_element_type=F32)


def dot_nt(a, b):
    return lax.dot_general(a, b, (((1,), (1,)), ((), ())), preferred_element_type=F32)


def dot_tn(a, b):
    return lax.dot_general(a, b, (((0,), (0,)), ((), ())), preferred_element_type=F32)


class Layer:
    def __init__(self, frames, side, halved):
        self.frames = frames
        self.side = side
        self.halved = halved
        self.frame = -(-side * side // 16) * 16
        self.rows = frames * self.frame

    def at(self, t):
        return slice(t * self.frame, (t + 1) * self.frame)


def point_a(layer, mask, x_ref, w_ref, za_ref, sums_ref):
    sums_ref[...] = jnp.zeros(sums_ref.shape, F32)
    for t in range(layer.frames):
        z = dot_nt(x_ref[layer.at(t), :], w_ref[...])
        za_ref[layer.at(t), :] = z
        for j in range(3):
            part = z[:, tile(j)] * mask
            add_sums(sums_ref, tile(j), part, part * z[:, tile(j)])
    cells = jnp.sum(mask, axis=0, keepdims=True) * layer.frames
    sums_ref[2:3, :] = jnp.broadcast_to(cells, (1, 384))


def point_b(layer, mask, x_ref, w_ref, zb_ref, sums_ref, around):
    sums_ref[...] = jnp.zeros(sums_ref.shape, F32)
    clear_edges(around, layer.frame)
    flat = []
    for t in range(layer.frames):
        z = dot(x_ref[layer.at(t), :], w_ref[...])
        zb_ref[layer.at(t), 0:256] = z[:, 0:256]
        zb_ref[layer.at(t), tile(2)] = z[:, tile(2)] * mask
        for j in range(2):
            part = z[:, tile(j)] * mask
            add_sums(sums_ref, tile(j), part, part * z[:, tile(j)])
    flat = [zb_ref[layer.at(t), tile(2)] for t in range(layer.frames)]

    def put(t, value):
        zb_ref[layer.at(t), tile(2)] = value
        part = value * mask
        add_sums(sums_ref, tile(2), part, part * value)

    neighbour_sum(flat, around, layer.frame, layer.side, put)


def first_a(layer, group_ref, sides_ref, x_ref, w_ref, za_ref, sums_ref):
    mask = crop_mask(layer.frame, layer.side, crop_of(group_ref, sides_ref, layer.halved))
    point_a(layer, mask, x_ref, w_ref, za_ref, sums_ref)


def first_b(layer, group_ref, sides_ref, x_ref, w_ref, zb_ref, sums_ref, around):
    mask = crop_mask(layer.frame, layer.side, crop_of(group_ref, sides_ref, layer.halved))
    point_b(layer, mask, x_ref, w_ref, zb_ref, sums_ref, around)


def conv_forward(
    layer, group_ref, sides_ref, za_ref, suma_ref, para_ref, sumb_ref, w_ref, wn_ref,
    wide_ref, thin_ref, zc_ref, sums_ref, around, rem,
):
    frames, frame, side = layer.frames, layer.frame, layer.side
    mask = crop_mask(frame, side, crop_of(group_ref, sides_ref, layer.halved))
    count = suma_ref[2:3, :]
    mean, inverse = moments(suma_ref, count)
    gain = para_ref[0:1, :] * inverse
    offset = para_ref[1:2, :] - mean * gain
    column = [column_mask(frame, side, dw) for dw in (-1, 0, 1)]
    part_of = lanes() // 32
    clear_edges(around, frame)
    for t in range(frames):
        rows = layer.at(t)
        for j in range(3):
            u = za_ref[rows, tile(j)] * gain[:, tile(j)] + offset[:, tile(j)]
            around[EDGE : EDGE + frame, tile(j)] = u * sigmoid(u) * mask
        mixed = {1: [None] * 3, 2: [None] * 3}
        for k, (dh, dw) in enumerate(TAPS):
            start = EDGE + dh * side + dw
            shifted = around[start : start + frame, tile(0)]
            if dw:
                shifted = shifted * column[dw + 1]
            wide_ref[rows, tile(k)] = shifted.astype(LOW)
            for j in (1, 2):
                shifted = around[start : start + frame, tile(j)]
                if dw:
                    shifted = shifted * column[dw + 1]
                shifted = jnp.where(part_of == k % 4, shifted, 0.0)
                held = mixed[j][k // 4]
                mixed[j][k // 4] = shifted if held is None else held + shifted
        for g in range(3):
            wide_ref[rows, tile(9 + g)] = mixed[1][g].astype(LOW)
            thin_ref[rows, tile(g)] = mixed[2][g].astype(LOW)
    sums_ref[:, 0:384] = sumb_ref[...]
    sums_ref[:, 384:896] = jnp.zeros((2, 512), F32)
    zc_ref[...] = jnp.zeros(zc_ref.shape, F32)
    for t in range(frames):
        source = wide_ref[layer.at(t), :]
        thin = thin_ref[layer.at(t), :]
        for k in range(3):
            to = t + 1 - k
            if 0 <= to < frames:
                rows = layer.at(to)
                zc_ref[rows, 0:256] += dot(source, w_ref[:, k * 256 : (k + 1) * 256])
                zc_ref[rows, tile(3)] += dot(thin, wn_ref[:, tile(k)])
        rem[layer.at(t), :] = dot(source, w_ref[:, 768:1024])
    for t in range(frames):
        rows = layer.at(t)
        total = pltpu.roll(rem[rows, 0:128], 64, 1)
        if t > 0:
            total = total + rem[layer.at(t - 1), 0:128]
        if t < frames - 1:
            total = total + rem[layer.at(t + 1), 128:256]
        zc_ref[rows, tile(2)] = jnp.where(lanes() < 64, total, 0.0)
        for j in range(4):
            z = zc_ref[rows, tile(j)]
            part = z * mask
            add_sums(sums_ref, tile(3 + j), part, part * z)


class Norms:
    def __init__(self, sums_ref, par_ref, count):
        mean, inverse = moments(sums_ref, count)
        self.mean, self.inverse = mean, inverse
        self.gamma, self.beta = par_ref[0:1, :], par_ref[1:2, :]

    def lane(self, kind, j):
        return tile(j if kind == "b" else 3 + j)

    def normed(self, z, at):
        return (z - self.mean[:, at]) * self.inverse[:, at]

    def shifted(self, n, at):
        return self.gamma[:, at] * n + self.beta[:, at]


def finish_lower(
    lower, upper, group_ref, sides_ref, zb_ref, zc_ref, suma_ref, sums_ref, par_ref, wa_ref, wb_ref,
    q_ref, za2_ref, zb2_ref, suma2_ref, sumb2_ref, around, y_ref,
):
    crop = crop_of(group_ref, sides_ref, False)
    mask = crop_mask(lower.frame, lower.side, crop)
    norms = Norms(sums_ref, par_ref, suma_ref[2:3, 0:1])
    pick = pair_matrix(upper, lower)
    for t in range(upper.frames):
        for index, (kind, j) in enumerate(UNIT_TILES):
            at = norms.lane(kind, j)
            z_ref = zb_ref if kind == "b" else zc_ref
            total = None
            for source in (2 * t, 2 * t + 1):
                u = norms.shifted(norms.normed(z_ref[lower.at(source), tile(j)], at), at)
                out = u * sigmoid(u) * mask
                total = out if total is None else total + out
            high = total.astype(LOW)
            y_ref[:, tile(index)] = high
            y_ref[:, tile(7 + index)] = (total - high.astype(F32)).astype(LOW)
        both = dot(pick, y_ref[...])
        q_ref[upper.at(t), :] = (both[:, 0:896] + both[:, 896:1792]).astype(LOW)
    small = crop_mask(upper.frame, upper.side, crop_of(group_ref, sides_ref, True))
    point_a(upper, small, q_ref, wa_ref, za2_ref, suma2_ref)
    point_b(upper, small, q_ref, wb_ref, zb2_ref, sumb2_ref, around)


def pair_matrix(upper, lower):
    at = lax.broadcasted_iota(jnp.int32, (upper.frame, lower.frame), 1).astype(F32)
    row = jnp.floor((at + 0.5) * (1.0 / lower.side))
    column = at - row * lower.side
    group = jnp.floor(row * 0.5 + 0.25) * upper.side + jnp.floor(column * 0.5 + 0.25)
    mine = lax.broadcasted_iota(jnp.int32, (upper.frame, lower.frame), 0).astype(F32)
    return jnp.where(jnp.abs(group - mine) < 0.5, 0.125, 0.0).astype(LOW)


def spread_matrix(upper, lower):
    at = lax.broadcasted_iota(jnp.int32, (lower.frame, upper.frame), 0).astype(F32)
    row = jnp.floor((at + 0.5) * (1.0 / lower.side))
    column = at - row * lower.side
    group = jnp.floor(row * 0.5 + 0.25) * upper.side + jnp.floor(column * 0.5 + 0.25)
    mine = lax.broadcasted_iota(jnp.int32, (lower.frame, upper.frame), 1).astype(F32)
    return jnp.where(jnp.abs(group - mine) < 0.5, 0.125, 0.0).astype(LOW)


def finish_upper(
    layer, group_ref, sides_ref, zb_ref, zc_ref, suma_ref, sums_ref, par_ref, cot_ref,
    out_ref, gu_ref, back_ref,
):
    mask = crop_mask(layer.frame, layer.side, crop_of(group_ref, sides_ref, layer.halved))
    norms = Norms(sums_ref, par_ref, suma_ref[2:3, 0:1])
    back_ref[...] = jnp.zeros(back_ref.shape, F32)
    for t in range(layer.frames):
        rows = layer.at(t)
        for index, (kind, j) in enumerate(UNIT_TILES):
            at = norms.lane(kind, j)
            z_ref = zb_ref if kind == "b" else zc_ref
            n = norms.normed(z_ref[rows, tile(j)], at)
            u = norms.shifted(n, at)
            s = sigmoid(u)
            out_ref[rows, tile(index)] = (u * s * mask).astype(LOW)
            gu = cot_ref[rows, tile(index)].astype(F32) * mask * (s * (1.0 + u * (1.0 - s)))
            gu_ref[rows, tile(index)] = gu
            add_sums(back_ref, at, gu, gu * n)


def unit_backward(
    layer, group_ref, sides_ref, gu_ref, zb_ref, zc_ref, suma_ref, sums_ref, back_ref, par_ref,
    dzb_ref, three_ref, thin3_ref, around, flat,
):
    frames, frame, side = layer.frames, layer.frame, layer.side
    mask = crop_mask(frame, side, crop_of(group_ref, sides_ref, layer.halved))
    count = suma_ref[2:3, 0:1]
    norms = Norms(sums_ref, par_ref, count)
    c0, c1, c2 = back_terms(back_ref, count, norms.gamma, norms.inverse)
    low_half = lanes() < 64

    def dz_of(t, index):
        kind, j = UNIT_TILES[index]
        at = norms.lane(kind, j)
        z_ref = zb_ref if kind == "b" else zc_ref
        rows = layer.at(t)
        n = norms.normed(z_ref[rows, tile(j)], at)
        return (gu_ref[rows, tile(index)] * c0[:, at] - c1[:, at] - n * c2[:, at]) * mask

    clear_edges(around, frame)
    for t in range(frames):
        for index in (0, 1):
            dzb_ref[layer.at(t), tile(index)] = dz_of(t, index).astype(LOW)
        flat[layer.at(t), :] = dz_of(t, 6)

    def put(t, value):
        dzb_ref[layer.at(t), tile(2)] = (value * mask).astype(LOW)

    neighbour_sum([flat[layer.at(t), :] for t in range(frames)], around, frame, side, put)
    for t in range(frames):
        flat[layer.at(t), :] = jnp.where(low_half, dz_of(t, 4), 0.0)
    empty = jnp.zeros((frame, 128), LOW)
    for t in range(frames):
        parts = [dz_of(t, index).astype(LOW) for index in (2, 3, 5)]
        for k in range(3):
            to = t - 1 + k
            if 0 <= to < frames:
                rows = layer.at(to)
                three_ref[rows, tile(2 * k)] = parts[0]
                three_ref[rows, tile(2 * k + 1)] = parts[1]
                thin3_ref[rows, tile(k)] = parts[2]
        rest = pltpu.roll(flat[layer.at(t), :], 64, 1)
        if t < frames - 1:
            rest = rest + flat[layer.at(t + 1), :]
        three_ref[layer.at(t), tile(6)] = rest.astype(LOW)
        three_ref[layer.at(t), tile(7)] = flat[layer.at(t - 1), :].astype(LOW) if t else empty
    for rows, k in ((layer.at(0), 2), (layer.at(frames - 1), 0)):
        three_ref[rows, tile(2 * k)] = empty
        three_ref[rows, tile(2 * k + 1)] = empty
        thin3_ref[rows, tile(k)] = empty


def conv_backward(
    layer, group_ref, sides_ref, three_ref, thin3_ref, za_ref, suma_ref, para_ref, wt_ref, wnt_ref,
    gua_ref, backa_ref, around, shifts, thins, rem, main,
):
    frames, frame, side = layer.frames, layer.frame, layer.side
    mask = crop_mask(frame, side, crop_of(group_ref, sides_ref, layer.halved))
    column = [column_mask(frame, side, dw) for dw in (-1, 0, 1)]
    low_half = lanes() < 64
    first_part = lanes() < 32
    clear_edges(around, frame)
    main[...] = jnp.zeros(main.shape, F32)
    rem[...] = jnp.zeros(rem.shape, F32)
    for t in range(frames):
        rows = layer.at(t)
        rest = jnp.where(low_half, 0.0, three_ref[rows, tile(6)].astype(F32))
        parts = [
            three_ref[rows, tile(2)].astype(F32),
            three_ref[rows, tile(3)].astype(F32),
            rest + pltpu.roll(rest, 64, 1),
            thin3_ref[rows, tile(1)].astype(F32),
        ]
        for j in range(4):
            around[EDGE : EDGE + frame, tile(j)] = parts[j]
        mixed = [None] * 5
        for k, (dh, dw) in enumerate(TAPS):
            start = EDGE - dh * side - dw
            for j in range(4):
                shifted = around[start : start + frame, tile(j)]
                if dw:
                    shifted = shifted * column[1 - dw]
                if j < 2:
                    shifts[:, tile(2 * k + j)] = shifted.astype(LOW)
                elif j == 3:
                    thins[:, tile(k)] = shifted.astype(LOW)
                else:
                    shifted = jnp.where(low_half if k % 2 == 0 else ~low_half, shifted, 0.0)
                    held = mixed[k // 2]
                    mixed[k // 2] = shifted if held is None else held + shifted
        for g in range(5):
            shifts[:, tile(18 + g)] = mixed[g].astype(LOW)
        product = dot_nt(shifts[...], wt_ref[...])
        thin = dot_nt(thins[...], wnt_ref[...])
        for k in range(3):
            to = t - 1 + k
            if 0 <= to < frames:
                rows = layer.at(to)
                main[rows, :] += product[:, tile(k)]
                turn = (128 - 32 * k) % 128
                last = product[:, tile(3)]
                rem[rows, 0:128] += last if turn == 0 else pltpu.roll(last, turn, 1)
                rem[rows, 128:256] += thin if turn == 0 else pltpu.roll(thin, turn, 1)
    mean, inverse = moments(suma_ref, suma_ref[2:3, :])
    backa_ref[...] = jnp.zeros(backa_ref.shape, F32)
    for t in range(frames):
        rows = layer.at(t)
        for j in range(3):
            grad = main[rows, :] if j == 0 else rem[rows, tile(j - 1)]
            n = (za_ref[rows, tile(j)] - mean[:, tile(j)]) * inverse[:, tile(j)]
            u = para_ref[0:1, tile(j)] * n + para_ref[1:2, tile(j)]
            s = sigmoid(u)
            gu = grad * mask * (s * (1.0 + u * (1.0 - s)))
            if j:
                gu = jnp.where(first_part, gu, 0.0)
            gua_ref[rows, tile(j)] = gu
            add_sums(backa_ref, tile(j), gu, gu * n)


def point_back(layer, mask, gua_ref, za_ref, suma_ref, backa_ref, para_ref, dza_ref):
    count = suma_ref[2:3, :]
    mean, inverse = moments(suma_ref, count)
    c0, c1, c2 = back_terms(backa_ref, count, para_ref[0:1, :], inverse)
    for t in range(layer.frames):
        rows = layer.at(t)
        for j in range(3):
            at = tile(j)
            n = (za_ref[rows, at] - mean[:, at]) * inverse[:, at]
            dz = (gua_ref[rows, at] * c0[:, at] - c1[:, at] - n * c2[:, at]) * mask
            if j:
                dz = jnp.where(lanes() < 32, dz, 0.0)
            dza_ref[rows, at] = dz.astype(LOW)


def join_blocks(
    upper, lower, group_ref, sides_ref, gua_ref, za_ref, suma_ref, backa_ref, para_ref, dzb_ref, wa_ref, wb_ref,
    zb_ref, zc_ref, suma1_ref, sums1_ref, par1_ref, dza_ref, gu_ref, back_ref, wide,
):
    small = crop_mask(upper.frame, upper.side, crop_of(group_ref, sides_ref, True))
    point_back(upper, small, gua_ref, za_ref, suma_ref, backa_ref, para_ref, dza_ref)
    mask = crop_mask(lower.frame, lower.side, crop_of(group_ref, sides_ref, False))
    norms = Norms(sums1_ref, par1_ref, suma1_ref[2:3, 0:1])
    back_ref[...] = jnp.zeros(back_ref.shape, F32)
    pick = spread_matrix(upper, lower)
    for t in range(upper.frames):
        rows = upper.at(t)
        dq = dot_nt(dzb_ref[rows, :], wb_ref[...]) + dot(dza_ref[rows, :], wa_ref[...])
        high = dq.astype(LOW)
        rest = (dq - high.astype(F32)).astype(LOW)
        wide[...] = dot(pick, high) + dot(pick, rest)
        for source in (2 * t, 2 * t + 1):
            at_rows = lower.at(source)
            for index, (kind, j) in enumerate(UNIT_TILES):
                at = norms.lane(kind, j)
                z_ref = zb_ref if kind == "b" else zc_ref
                n = norms.normed(z_ref[at_rows, tile(j)], at)
                u = norms.shifted(n, at)
                s = sigmoid(u)
                gu = wide[:, tile(index)] * mask * (s * (1.0 + u * (1.0 - s)))
                gu_ref[at_rows, tile(index)] = gu
                add_sums(back_ref, at, gu, gu * n)


def last_back(
    layer, group_ref, sides_ref, gua_ref, za_ref, suma_ref, backa_ref, para_ref, dzb_ref, wa_ref, wb_ref, dza_ref, grad_ref,
):
    mask = crop_mask(layer.frame, layer.side, crop_of(group_ref, sides_ref, layer.halved))
    point_back(layer, mask, gua_ref, za_ref, suma_ref, backa_ref, para_ref, dza_ref)
    for t in range(layer.frames):
        rows = layer.at(t)
        total = dot_nt(dzb_ref[rows, :], wb_ref[...]) + dot(dza_ref[rows, :], wa_ref[...])
        grad_ref[rows, :] = (total * mask).astype(LOW)


def place(me, pair, core):
    bits = lax.shift_right_logical(me, 1) ^ pair
    x, y = bits & 1, lax.shift_right_logical(bits, 1) & 1
    near, far = lax.shift_right_logical(bits, 2) & 1, lax.shift_right_logical(bits, 3) & 1
    first = x + core * (y - x)
    second = y + core * (x - y)
    return first * 8 + second * 4 + near * 2 + far


def put_pair(me, keep_ref, send_ref, pair, rows, even, odd):
    core = me & 1
    mine = core == 0
    keep_ref[place(me, pair, core), rows, :] = jnp.where(mine, even, odd)
    send_ref[place(me, pair, 1 - core), rows, :] = jnp.where(mine, odd, even)


def get_pair(me, own_ref, other_ref, pair, rows):
    core = me & 1
    mine = core == 0
    own = own_ref[place(me, pair, core), rows, :]
    other = other_ref[place(me, pair, 1 - core), rows, :]
    return jnp.where(mine, own, other), jnp.where(mine, other, own)


def segments(blocks):
    rows = -(-sum(length for _, length in blocks) // 256) * 8
    pieces, piece, room = [], [], rows
    for name, length in blocks:
        at = 0
        while at < length:
            take = min(room, length - at)
            piece.append((name, at, at + take, rows - room))
            at += take
            room -= take
            if not room:
                pieces.append(piece)
                piece, room = [], rows
    if piece:
        pieces.append(piece)
    return rows, pieces + [[]] * (32 - len(pieces))


def wide(layer, *tiles):
    return [(("wide", j, layer), 1440) for j in tiles]


def point_and_thin(layer):
    return [(("point", j, layer), 832) for j in range(3)] + [(("thin", j, layer), 288) for j in range(3)]


def last(layer):
    return [(("last", j, layer), 192) for j in range(7)]


PARTS = [
    segments(wide(1, *range(8)) + point_and_thin(1)),
    segments(wide(0, 0, 1, 2, 3, 6) + last(1)),
    segments(wide(0, 4, 5, 7) + point_and_thin(0)),
    segments(last(0)),
]


def joined_part(first, second):
    rows = first[0]
    pieces = [a + [(name, low, end, row + rows) for name, low, end, row in b] for a, b in zip(first[1], second[1])]
    return rows + second[0], pieces


def piece_value(piece, rows, read):
    parts = [read(name, first, end) for name, first, end, _ in piece]
    filled = sum(end - first for _, first, end, _ in piece)
    if filled < rows:
        parts.append(jnp.zeros((rows - filled, 128), F32))
    return parts[0] if len(parts) == 1 else jnp.concatenate(parts, axis=0)


def put_pieces(me, keep_ref, send_ref, part, read):
    rows, pieces = part
    for pair in range(16):
        even, odd = (piece_value(pieces[2 * pair + i], rows, read) for i in (0, 1))
        put_pair(me, keep_ref, send_ref, pair, slice(0, rows), even, odd)


def without_gap(ref, grad):
    if grad.shape[0] == 896:
        ref[0:576, :] = grad[0:576]
        ref[576:832, :] = grad[640:896]
    else:
        ref[...] = grad


def weights(part, columns, kinds, me_ref, *refs):
    refs = list(refs)
    read_from = {}
    operands = [refs.pop(0) for _ in range({"w": 2, "o": 4, "l": 2}[kinds[0]] + (0 if len(kinds) == 1 else {"o": 4, "l": 2}[kinds[1]]))]
    keep_ref, send_ref = refs.pop(0), refs.pop(0)
    for kind in kinds:
        if kind == "w":
            wide_ref, three_ref = operands.pop(0), operands.pop(0)
            grad = refs.pop(0)
            at = 0
            for first, count in columns:
                grad[:, tile(at, count)] = dot_tn(wide_ref[:, 0:1440], three_ref[:, tile(first, count)])
                for j in range(count):
                    read_from["wide", first + j] = (grad, at + j)
                at += count
        elif kind == "o":
            thin_ref, thin3_ref, x_ref, dzb_ref = (operands.pop(0) for _ in range(4))
            thin_grad, point_grad = refs.pop(0), refs.pop(0)
            thin_grad[...] = dot_tn(thin_ref[...], thin3_ref[...])
            without_gap(point_grad, dot_tn(x_ref[...], dzb_ref[...]))
            for j in range(3):
                read_from["point", j] = (point_grad, j)
                read_from["thin", j] = (thin_grad, j)
        else:
            dza_ref, x_ref = operands.pop(0), operands.pop(0)
            last_grad = refs.pop(0)
            grad = dot_tn(dza_ref[...], x_ref[...])
            if grad.shape[1] == 896:
                grad = close_gap(grad)
            width = grad.shape[1]
            last_grad[0:160, 0:width] = grad[0:160]
            last_grad[160:192, 0:width] = grad[256:288]
            if width < 896:
                last_grad[:, width:896] = jnp.zeros((192, 896 - width), F32)
            for j in range(7):
                read_from["last", j] = (last_grad, j)

    def read(name, first, end):
        ref, j = read_from[name[0:2]]
        return ref[first:end, tile(j)]

    put_pieces(me_ref[0], keep_ref, send_ref, part, read)


OUT_SHAPES = [(832, 256), (160, 832), (27, 160, 320), (32, 832), (27, 32, 128), (832, 128)]
SINGLE, REDUCE, SPATIAL, SQUEEZE, NARROW, PROJECT = range(6)


def assemble(sources, targets, aliased, me_ref, *refs):
    me = me_ref[0]
    many = sum(2 if relative else 1 for _, relative in sources)
    arrived, refs = list(refs[0:many]), refs[many + (6 if aliased else 0) :]
    outs, stages, sems = refs[0:6], refs[6 : 6 + len(targets)], refs[6 + len(targets)]
    stage = {(which, block): (ref, first) for (which, block, first, _), ref in zip(targets, stages)}

    def put_wide(block, k, lanes_at, first, value):
        ref, offset = stage[SPATIAL, block]
        done = 0
        while done < value.shape[0]:
            row = first + done
            if row < 1152:
                tap, channel = row // 128, row % 128
                take = min(128 - channel, value.shape[0] - done)
            else:
                tap, channel = (row - 1152) // 32, 128 + (row - 1152) % 32
                take = min(160 - channel, value.shape[0] - done)
            ref[k * 9 + tap - offset, channel : channel + take, lanes_at] = value[done : done + take]
            done += take

    def put(name, first, end, value):
        kind, j, block = name
        if kind == "wide":
            if j < 6:
                put_wide(block, j // 2, tile(j % 2), first, value)
            elif j == 6:
                put_wide(block, 0, slice(256, 320), first, value[:, 0:64])
                put_wide(block, 1, slice(256, 320), first, pltpu.roll(value, 64, 1)[:, 0:64])
            else:
                put_wide(block, 2, slice(256, 320), first, value[:, 0:64])
        elif kind == "point":
            if j < 2:
                stage[SINGLE, block][0][first:end, tile(j)] = value
            else:
                stage[PROJECT, block][0][first:end, :] = value
        elif kind == "thin":
            done = 0
            while done < end - first:
                tap, channel = (first + done) // 32, (first + done) % 32
                take = min(32 - channel, end - first - done)
                stage[NARROW, block][0][j * 9 + tap, channel : channel + take, :] = value[done : done + take]
                done += take
        else:
            lanes_at = tile(j) if j < 6 else slice(768, 832)
            for which, low, high in ((REDUCE, 0, 160), (SQUEEZE, 160, 192)):
                begin, stop = max(first, low), min(end, high)
                if begin < stop:
                    part = value[begin - first : stop - first]
                    stage[which, block][0][begin - low : stop - low, lanes_at] = part if j < 6 else part[:, 0:64]

    for (rows, pieces), relative in sources:
        held = [arrived.pop(0) for _ in range(2 if relative else 1)]
        for pair in range(16):
            if relative:
                both = get_pair(me, *held, pair, slice(0, rows))
            else:
                both = [held[0][2 * pair + i] for i in (0, 1)]
            for i in (0, 1):
                for name, first, end, row in pieces[2 * pair + i]:
                    put(name, first, end, both[i][row : row + end - first])
    copies = []
    for i, ((which, block, first, count), ref) in enumerate(zip(targets, stages)):
        to = outs[which].at[block]
        if count < OUT_SHAPES[which][0]:
            to = to.at[pl.ds(first, count)]
        copies.append(pltpu.make_async_copy(ref, to, sems.at[i]))
        copies[-1].start()
    for copy in copies:
        copy.wait()


def assemble_call(me, sources, targets, outs):
    anywhere = pl.BlockSpec(memory_space=pl.ANY)
    arrays = sum((list(found) for _, found in sources), [])
    targets = [(which, block, first, count or OUT_SHAPES[which][0]) for which, block, first, count in targets]
    scratch = [pltpu.VMEM((count,) + OUT_SHAPES[which][1:], F32) for which, _, _, count in targets]
    return pl.pallas_call(
        functools.partial(assemble, [(part, len(found) == 2) for part, found in sources], targets, outs is not None),
        out_shape=tuple(struct((2,) + shape, F32) for shape in OUT_SHAPES),
        in_specs=[SMEM] + [VMEM] * len(arrays) + [anywhere] * (0 if outs is None else 6),
        out_specs=tuple([anywhere] * 6),
        scratch_shapes=scratch + [pltpu.SemaphoreType.DMA((len(targets),))],
        input_output_aliases={} if outs is None else {1 + len(arrays) + i: i for i in range(6)},
        compiler_params=pltpu.CompilerParams(vmem_limit_bytes=scoped(scratch, 8)),
        cost_estimate=pl.CostEstimate(
            flops=0, bytes_accessed=2 * scoped(scratch, 0), transcendentals=0
        ),
        name="assemble",
    )(me, *arrays, *([] if outs is None else outs))


def unfit_vectors(sums_a, sums):
    return jnp.concatenate(
        [sums[:, 0:256], sums_a[:, 0:160], sums[:, 384:704], sums_a[:, 256:288], sums[:, 768:896], sums[:, 256:384]], axis=1
    )


def open_gap(value):
    value = value.astype(F32)
    tiles = [value[:, tile(j)] for j in range(6)]
    tiles.append(jnp.concatenate([value[:, 768:832], jnp.zeros((value.shape[0], 64), F32)], axis=1))
    low_half = lanes() < 64
    turned = [pltpu.roll(part, 64, 1) for part in tiles[4:7]]
    tiles[4] = jnp.where(low_half, tiles[4], 0.0)
    tiles[5] = jnp.where(low_half, turned[0], turned[1])
    tiles[6] = jnp.where(low_half, turned[1], turned[2])
    return jnp.concatenate(tiles, axis=1).astype(LOW)


def close_gap(value):
    low_half = lanes() < 64
    tiles = [value[:, tile(j)] for j in range(7)]
    turned = [pltpu.roll(part, 64, 1) for part in tiles[5:7]]
    tiles[4] = jnp.where(low_half, tiles[4], turned[0])
    tiles[5] = jnp.where(low_half, turned[0], turned[1])
    tiles[6] = turned[1]
    return jnp.concatenate(tiles, axis=1)


def fit_points(single_ref, project_ref, reduce_ref, squeeze_ref, wa_ref, wb_ref):
    gap = wa_ref.shape[1] == 896
    if gap:
        spans = [(slice(0, 576), slice(0, 576)), (slice(640, 896), slice(576, 832))]
        wb_ref[576:640, :] = jnp.zeros((64, 384), LOW)
    else:
        spans = [(slice(0, 832), slice(0, 832))]
    for to, source in spans:
        wb_ref[to, 0:256] = single_ref[0, source, :]
        wb_ref[to, 256:384] = project_ref[0, source, :]
    reduce, squeeze = reduce_ref[0], squeeze_ref[0]
    if gap:
        reduce, squeeze = open_gap(reduce), open_gap(squeeze)
    wa_ref[0:128, :] = reduce[0:128]
    for i in range(4):
        wa_ref[128 + 32 * i : 160 + 32 * i, :] = reduce[128:160]
        wa_ref[256 + 32 * i : 288 + 32 * i, :] = squeeze


def pair_lanes(left, right):
    parts = [jnp.zeros((max(p.shape[0] for p in (left, right) if p is not None), 64), F32) if p is None else p.astype(F32) for p in (left, right)]
    return jnp.concatenate(parts, axis=1).astype(LOW)


def fit_convs(
    index, scale_ref, shift_ref, spatial_ref, narrow_ref, w_ref, wn_ref, wt_ref, wnt_ref, para_ref, par_ref
):
    spans = [(0, 128, 128 * tap, tap) for tap in range(9)] + [(128, 160, 1152 + 32 * tap, tap) for tap in range(9)]
    w_ref[1440:1536, :] = jnp.zeros((96, 1024), LOW)
    for first, end, row, tap in spans:
        rows = slice(row, row + end - first)
        rest = [spatial_ref[0, 9 * k + tap, first:end, 256:320] for k in range(3)]
        for k in range(3):
            w_ref[rows, k * 256 : (k + 1) * 256] = spatial_ref[0, 9 * k + tap, first:end, 0:256]
        w_ref[rows, 768:896] = pair_lanes(rest[0], rest[1])
        w_ref[rows, 896:1024] = pair_lanes(rest[2], None)
    wt_ref[480:512, :] = jnp.zeros((32, 2944), LOW)
    for k in range(3):
        for first, end, row in ((0, 128, 128 * k), (128, 160, 384 + 32 * k)):
            rows = slice(row, row + end - first)
            for tap in range(9):
                wt_ref[rows, tap * 256 : (tap + 1) * 256] = spatial_ref[0, 9 * k + tap, first:end, 0:256]
            for g in range(5):
                left = spatial_ref[0, 9 * k + 2 * g, first:end, 256:320]
                right = spatial_ref[0, 9 * k + 2 * g + 1, first:end, 256:320] if g < 4 else None
                wt_ref[rows, tile(18 + g)] = pair_lanes(left, right)
    wn_ref[288:384, :] = jnp.zeros((96, 384), LOW)
    wnt_ref[96:128, :] = jnp.zeros((32, 1152), LOW)
    for k in range(3):
        for tap in range(9):
            part = narrow_ref[0, 9 * k + tap]
            wn_ref[32 * tap : 32 * tap + 32, tile(k)] = part
            wnt_ref[32 * k : 32 * k + 32, tile(tap)] = part
    for row, ref in ((0, scale_ref), (1, shift_ref)):
        vector = ref[index : index + 1, :]
        rest = vector[:, 384:416]
        squeeze = vector[:, 736:768]
        para_ref[row : row + 1, 0:128] = vector[:, 256:384]
        para_ref[row : row + 1, 128:256] = jnp.concatenate([rest] * 4, axis=1)
        para_ref[row : row + 1, 256:384] = jnp.concatenate([squeeze] * 4, axis=1)
        par_ref[row : row + 1, 0:256] = vector[:, 0:256]
        par_ref[row : row + 1, 256:384] = vector[:, 896:1024]
        par_ref[row : row + 1, 384:768] = jnp.concatenate([vector[:, 416:736], jnp.zeros((1, 64), F32)], axis=1)
        par_ref[row : row + 1, 768:896] = vector[:, 768:896]


def fetch_block(body, index, held, made, *refs):
    whole, refs = refs[0 : len(refs) - 2 * held - made - 1], refs[len(refs) - 2 * held - made - 1 :]
    split, outs, parts, sems = refs[0:held], refs[held : held + made], refs[held + made : -1], refs[-1]
    copies = [pltpu.make_async_copy(ref.at[pl.ds(index, 1)], part, sems.at[i]) for i, (ref, part) in enumerate(zip(split, parts))]
    for copy in copies:
        copy.start()
    for copy in copies:
        copy.wait()
    body(*whole, *parts, *outs)


def layer_call(body, index, split, whole, outs, name=None):
    scratch = [pltpu.VMEM((1,) + x.shape[1:], x.dtype) for x in split]
    return pl.pallas_call(
        functools.partial(fetch_block, body, index, len(split), len(outs)),
        out_shape=tuple(outs),
        in_specs=[VMEM] * len(whole) + [pl.BlockSpec(memory_space=pl.ANY)] * len(split),
        out_specs=tuple([VMEM] * len(outs)),
        scratch_shapes=scratch + [pltpu.SemaphoreType.DMA((len(split),))],
        compiler_params=pltpu.CompilerParams(vmem_limit_bytes=scoped(scratch, 4)),
        cost_estimate=pl.CostEstimate(
            flops=0, bytes_accessed=2 * sum(x.size * x.dtype.itemsize for x in outs), transcendentals=0
        ),
        name=name,
    )(*whole, *split)


def exchange(value, sizes, bits):
    total = sizes[0] * sizes[1]

    def swap(mask):
        return lax.ppermute(value, AXES, [(i, i ^ mask) for i in range(total)])

    if len(bits) == 1:
        return value + swap(1 << bits[0])
    one, two = 1 << bits[0], 1 << bits[1]
    return (value + swap(one)) + (swap(two) + swap(one | two))


class Sum:
    def __init__(self, value, sizes):
        self.value, self.sizes, self.at = value, sizes, 0
        total = sizes[0] * sizes[1]
        bits = list(range(total.bit_length() - 1))
        self.stages = [bits[:1]] + [bits[at : at + 2] for at in range(1, len(bits), 2)]
        self.able = not (total & (total - 1))
        if not self.able:
            self.stages = []
            self.value = lax.psum(value, AXES)

    def step(self):
        if self.at < len(self.stages):
            self.value = exchange(self.value, self.sizes, self.stages[self.at])
            self.at += 1
        return self.value

    def result(self):
        while self.at < len(self.stages):
            self.step()
        return self.value


def sum_all(value, sizes):
    return Sum(value, sizes).result()


def meet(*holders):
    names = ("value",), ("keep", "send"), ("array",)
    found = [next(n for n in names if hasattr(holder, n[0])) for holder in holders]
    values = lax.optimization_barrier([[getattr(h, n) for n in ns] for h, ns in zip(holders, found)])
    for holder, ns, got in zip(holders, found, values):
        for n, value in zip(ns, got):
            setattr(holder, n, value)


class Held:
    def __init__(self, array):
        self.array = array


class Sharing:
    def __init__(self, sizes):
        dp, rep = sizes
        self.sizes = sizes
        self.total = dp * rep
        self.able = not (self.total & (self.total - 1)) and dp >= 8 and rep >= 4
        low = rep.bit_length() - 1
        self.bits = [0, 1, low, low + 1, low + 2]
        self.other = [bit for bit in range(self.total.bit_length() - 1) if bit not in self.bits]

    def me(self):
        if not self.able:
            return jnp.zeros((1,), jnp.int32)
        flat = lax.axis_index("dp") * self.sizes[1] + lax.axis_index("rep")
        index = sum(((flat >> bit) & 1) << i for i, bit in enumerate(self.bits))
        return index.reshape(1).astype(jnp.int32)

    def swap(self, value, even, odd=None):
        masks = [sum(1 << self.bits[i] for i in bits) for bits in (even, even if odd is None else odd)]
        return lax.ppermute(value, AXES, [(i, i ^ masks[i & 1]) for i in range(self.total)])

    def chain(self, keep, send):
        return Chain(self, keep, send)


class Chain:
    def __init__(self, sharing, keep, send, short=False):
        self.sharing, self.keep, self.send, self.stage = sharing, keep, send, 0
        self.short = short
        if not sharing.able:
            self.keep, self.send = lax.psum(keep, AXES), lax.psum(send, AXES)

    def step(self):
        if not self.sharing.able:
            return
        swap = self.sharing.swap
        send = self.send
        if self.short and self.stage == 1:
            kept = self.keep
            got = [swap(send[0:4], (1,), (2,)), swap(kept[4:8], (2,), (1,)), swap(send[4:8], (1, 2))]
            parts = [(kept[i] + got[0][i]) + (got[1][i] + got[2][i]) for i in range(4)]
            self.keep, self.send = parts[0], parts[1:]
            self.stage += 1
        elif self.short and self.stage == 5:
            self.send = jnp.concatenate([send, swap(send, (2,), (1,)), swap(send, (1,), (2,)), swap(send, (1, 2))])
            self.stage += 1
        elif self.stage < 3:
            got = swap(send, *(((0,),), ((1,), (2,)), ((2,), (1,)))[self.stage])
            half = 8 >> self.stage
            if self.stage < 2:
                self.keep, self.send = self.keep[0:half] + got[0:half], self.keep[half:] + got[half:]
            else:
                parts = [self.keep[i] + got[i] for i in range(4)]
                self.keep, self.send = parts[0], parts[1:]
        elif self.stage == 3:
            got = [swap(send[0], (4,)), swap(send[1], (3,)), swap(send[2], (3, 4))]
            whole = (self.keep + got[0]) + (got[1] + got[2])
            for bit in self.sharing.other:
                whole = exchange(whole, self.sharing.sizes, [bit])
            self.send = whole
            self.keep = ()
            self.whole = True
        elif self.stage == 4:
            self.send = jnp.stack([send, swap(send, (4,)), swap(send, (3,)), swap(send, (3, 4))])
        elif self.stage < 7:
            self.send = jnp.concatenate([send, swap(send, *(((2,), (1,)), ((1,), (2,)))[self.stage - 5])])
        else:
            self.keep, self.send = send, swap(send, (0,))
        self.stage += 1

    def join(self, other):
        if self.sharing.able:
            self.send = jnp.concatenate([self.send, other.send], axis=0)
        else:
            self.keep = jnp.concatenate([self.keep, other.keep], axis=1)
            self.send = jnp.concatenate([self.send, other.send], axis=1)

    def result(self):
        return [self.keep, self.send]


def shards(sizes, *arguments):
    clip_input, cotangent, clip_group, crop_sides = arguments[:4]
    kernels, bn_scale, bn_shift = arguments[4:10], arguments[10], arguments[11]
    w_single, w_reduce, w_spatial, w_squeeze, w_narrow, w_project = kernels
    _, frames, side, _, width = clip_input.shape
    lower, upper = Layer(frames, side, False), Layer(frames // 2, side // 2, True)
    where = [clip_group, crop_sides]
    merged = [w_spatial.reshape(2, 27, 160, 320), w_narrow.reshape(2, 27, 32, 128)]
    turned = [jnp.swapaxes(w_reduce, 1, 2), jnp.swapaxes(w_squeeze, 1, 2)]
    points = [
        layer_call(
            fit_points, i, [w_single, w_project] + turned, [],
            [struct((384, 832 + 64 * i), LOW), struct((832 + 64 * i, 384), LOW)], name="fit_points",
        )
        for i in (0, 1)
    ]
    fitted = [
        layer_call(
            functools.partial(fit_convs, i),
            i,
            merged,
            [bn_scale, bn_shift],
            [struct((1536, 1024), LOW), struct((384, 384), LOW), struct((512, 2944), LOW), struct((128, 1152), LOW)]
            + [struct((2, 384), F32), struct((2, 896), F32)],
            name="fit_convs",
        )
        for i in (0, 1)
    ]
    pars = [item[4:6] for item in fitted]
    spatials = [(item[0], item[2]) for item in fitted]
    narrows = [(item[1], item[3]) for item in fitted]
    def frames_first(value, layer):
        value = jnp.transpose(value, (0, 2, 3, 1, 4)).reshape(layer.side * layer.side, layer.frames, width)
        return jnp.transpose(value, (1, 0, 2))

    def frames_back(value, layer):
        value = jnp.transpose(value, (1, 0, 2)).reshape(1, layer.side, layer.side, layer.frames, width)
        return jnp.transpose(value, (0, 3, 1, 2, 4))

    x = frames_first(clip_input, lower).reshape(lower.rows, width)
    cot = frames_first(cotangent, upper)
    cot = jnp.concatenate(
        [cot[..., 0:576], jnp.zeros(cot.shape[:2] + (64,), LOW), cot[..., 576:832]], axis=2
    )
    cot = jnp.pad(cot, ((0, 0), (0, upper.frame - upper.side * upper.side), (0, 0))).reshape(upper.rows, 896)

    def around(layer, tiles):
        return pltpu.VMEM((layer.frame + 2 * EDGE, 128 * tiles), F32)

    def forward(layer, za, suma, sumb, index):
        r = layer.rows
        return call(
            functools.partial(conv_forward, layer),
            where + [za, suma, pars[index][0], sumb, spatials[index][0], narrows[index][0]],
            [struct((r, 1536), LOW), struct((r, 384), LOW), struct((r, 512), F32), struct((2, 896), F32)],
            [around(layer, 3), pltpu.VMEM((r, 256), F32)],
            flops=2 * r * 27 * 160 * 320,
            name="conv_forward",
        )

    def unit_back(layer, gu, zb, zc, suma, sums, back, index):
        r = layer.rows
        return call(
            functools.partial(unit_backward, layer),
            where + [gu, zb, zc, suma, sums, back, pars[index][1]],
            [struct((r, 384), LOW), struct((r, 1024), LOW), struct((r, 384), LOW)],
            [around(layer, 1), pltpu.VMEM((r, 128), F32)],
            name="unit_backward",
        )

    def conv_back(layer, three, thin3, za, suma, index):
        r = layer.rows
        return call(
            functools.partial(conv_backward, layer),
            where + [three, thin3, za, suma, pars[index][0], spatials[index][1], narrows[index][1]],
            [struct((r, 384), F32), struct((2, 384), F32)],
            [
                around(layer, 4),
                pltpu.VMEM((layer.frame, 2944), LOW),
                pltpu.VMEM((layer.frame, 1152), LOW),
                pltpu.VMEM((r, 256), F32),
                pltpu.VMEM((r, 128), F32),
            ],
            flops=2 * r * 27 * 160 * 320,
            name="conv_backward",
        )

    sharing = Sharing(sizes)
    me = sharing.me()

    def make_weights(index, columns, kinds, *operands, short=False):
        part = PARTS[index]
        scratch = []
        for kind in kinds:
            if kind == "w":
                scratch.append((1440, 128 * sum(count for _, count in columns)))
            elif kind == "o":
                scratch += [(384, 384), (832, 384)]
            else:
                scratch.append((192, 896))
        made = call(
            functools.partial(weights, part, columns, kinds),
            [me, *operands],
            [struct((16, part[0], 128), F32)] * 2,
            [pltpu.VMEM(shape, F32) for shape in scratch],
            scalars=1,
            flops=2 * operands[0].shape[0] * 32 * part[0] * 128,
            name="weights",
        )
        return Chain(sharing, *made, short=short)

    r0, r1 = lower.rows, upper.rows
    za, suma = call(
        functools.partial(first_a, lower), where + [x, points[0][0]],
        [struct((r0, 384), F32), struct((3, 384), F32)], flops=2 * r0 * 832 * 384, name="first_a",
    )
    suma = sum_all(suma, sizes)
    zb, sumb = call(
        functools.partial(first_b, lower), where + [x, points[0][1]],
        [struct((r0, 384), F32), struct((2, 384), F32)], [around(lower, 1)], flops=2 * r0 * 832 * 384, name="first_b",
    )
    wide, thin, zc, sums = forward(lower, za, suma, sumb, 0)
    sums = sum_all(sums, sizes)
    q, za2, zb2, suma2, sumb2 = call(
        functools.partial(finish_lower, lower, upper),
        where + [zb, zc, suma, sums, pars[0][1], *points[1]],
        [struct((r1, 896), LOW), struct((r1, 384), F32), struct((r1, 384), F32), struct((3, 384), F32), struct((2, 384), F32)],
        [around(upper, 1), pltpu.VMEM((lower.frame, 1792), LOW)],
        flops=2 * r1 * 832 * 768,
        name="finish_lower",
    )
    suma2 = sum_all(suma2, sizes)
    wide2, thin2, zc2, sums2 = forward(upper, za2, suma2, sumb2, 1)
    sums2 = sum_all(sums2, sizes)
    out, gu2, back2 = call(
        functools.partial(finish_upper, upper),
        where + [zb2, zc2, suma2, sums2, pars[1][1], cot],
        [struct((r1, 896), LOW), struct((r1, 896), F32), struct((2, 896), F32)],
        name="finish_upper",
    )
    back2 = sum_all(back2, sizes)
    dzb2, three2, thin32 = unit_back(upper, gu2, zb2, zc2, suma2, sums2, back2, 1)
    gua2, backa2 = conv_back(upper, three2, thin32, za2, suma2, 1)
    small = Sum(backa2, sizes)
    small.step()
    one = make_weights(0, [(0, 2), (2, 2), (4, 2), (6, 2)], "wo", wide2, three2, thin2, thin32, q, dzb2)
    meet(small, one)
    small.step()
    one.step()
    meet(small, one)
    backa2 = small.result()
    one.step()
    dza2, gu, back = call(
        functools.partial(join_blocks, upper, lower),
        where + [gua2, za2, suma2, backa2, pars[1][0], dzb2, *points[1], zb, zc, suma, sums, pars[0][1]],
        [struct((r1, 384), LOW), struct((r0, 896), F32), struct((2, 896), F32)],
        [pltpu.VMEM((lower.frame, 896), F32)],
        flops=2 * r1 * 832 * 768,
        name="join_blocks",
    )
    held = Held(sum_all(back, sizes))
    meet(held, one)
    back = held.array
    one.step()
    dzb, three, thin3 = unit_back(lower, gu, zb, zc, suma, sums, back, 0)
    two = make_weights(1, [(0, 2), (2, 2), (6, 1)], "wl", wide, three, dza2, q)
    held = Held(three)
    meet(one, two, held)
    one.step()
    two.step()
    two.step()
    gua, backa = conv_back(lower, held.array, thin3, za, suma, 0)
    held = Held(three), Held(backa)
    meet(two, *held)
    more = make_weights(2, [(4, 2), (7, 1)], "wo", wide, held[0].array, thin, thin3, x, dzb)
    meet(one, more)
    one.step()
    two.step()
    more.step()
    more.step()
    backa = sum_all(held[1].array, sizes)
    dza, da = call(
        functools.partial(last_back, lower),
        where + [gua, za, suma, backa, pars[0][0], dzb, *points[0]],
        [struct((r0, 384), LOW), struct((r0, 832), LOW)],
        flops=2 * r0 * 832 * 768,
        name="last_back",
    )
    final = make_weights(3, [], "l", dza, x, short=True)
    meet(one, two, more, final)
    one.step()
    two.step()
    more.step()
    final.step()
    final.step()
    da = Held(frames_back(da.reshape(lower.frames, lower.frame, width), lower))
    out = jnp.concatenate([out[:, 0:576], out[:, 640:896]], axis=1)
    out = out.reshape(upper.frames, upper.frame, width)[:, 0 : upper.side * upper.side]
    out = Held(frames_back(out, upper))
    meet(one, two, more, final, da, out)
    one.step()
    two.step()
    more.step()
    final.step()
    meet(one, two, more, final)
    more.join(final)
    one.step()
    two.step()
    two.step()
    more.step()
    meet(one, two, more)
    joined = Held(assemble_call(me, [(PARTS[0], one.result())], [(which, 1, 0, 0) for which in (SINGLE, SPATIAL, NARROW, PROJECT)], None))
    two.step()
    more.step()
    more.step()
    meet(two, more, joined)
    joined.array = assemble_call(
        me, [(PARTS[1], two.result())], [(SPATIAL, 0, 0, 18), (REDUCE, 1, 0, 0), (SQUEEZE, 1, 0, 0)], list(joined.array)
    )
    more.step()
    meet(more, joined)
    joined = list(joined.array)
    joined = list(assemble_call(
        me,
        [(joined_part(PARTS[2], PARTS[3]), more.result())],
        [(SPATIAL, 0, 18, 9)] + [(which, 0, 0, 0) for which in (SINGLE, REDUCE, SQUEEZE, NARROW, PROJECT)],
        joined,
    ))
    joined[REDUCE], joined[SQUEEZE] = (jnp.swapaxes(joined[which], 1, 2) for which in (REDUCE, SQUEEZE))
    joined = [value.reshape(kernel.shape) for value, kernel in zip(joined, kernels)]
    both = jnp.stack([unfit_vectors(backa, back), unfit_vectors(backa2, back2)])
    return (
        out.array,
        da.array,
        *joined,
        both[:, 1],
        both[:, 0],
    )


def solution(mesh):
    split = P(AXES, None, None, None, None)
    sizes = tuple(mesh.shape[axis] for axis in AXES)
    return jax.shard_map(
        functools.partial(shards, sizes),
        mesh=mesh,
        in_specs=(split, split, P(AXES)) + (P(),) * 9,
        out_specs=(split, split) + (P(),) * 8,
        check_vma=False,
    )
```

profile of v0, /device:TPU:0, one launch (start us, length us, event | category | flops | bytes accessed | tf_op | source)
XLA Modules:
  0.0 375.2 jit_solution(1975345159860047118)
XLA Ops:
  1.3 2.3 copy.34
  4.6 2.4 first_a.1
  8.4 3.8 %collective-permute-start.3 = (f32[3,384]{1,0:T(4,128)S(1)}, f32[3,384]{1,0:T(4,128)S(1)}, u32[]{:S(2)}, u32[]{:S(2)}) collective-permute-start(f32[3,384]{1,0:T(4,128)S(1)} %add.391), channel_id=1, source_target_pairs={{0,6},{1,7},{2,4},{3,5},{4,2},{5,3},{6,0},{7,1},{8,14},{9,15},{10,... | collective-permute-start | bytes 13832 | tf_op jit(solution)/shard_map/ppermute | solution.py:879
  16.3 3.6 collective-permute-start.6
  20.7 2.9 first_b.1
  28.0 10.7 %conv_forward.2 = (bf16[1600,1536]{1,0:T(8,128)(2,1)S(1)}, bf16[1600,384]{1,0:T(8,128)(2,1)S(1)}, f32[1600,512]{1,0:T(8,128)S(1)}, f32[2,896]{1,0:T(2,128)S(1)}) custom-call(s32[1]{0:T(128)S(6)} %copy.57.group_ref, s32[3]{0:T(128)S(1)} %copy-done.37, f32[1600,384]{1,0:T(8,128)S(1)} %get-tuple-element.159.za_ref, ...), custom_call_target="tpu_custom_call" | custom-call | flops 4423680000 | bytes 5909008 | tf_op jit(solution)/shard_map/conv_forward/pallas_call | solution.py:39
  47.7 3.8 %collective-permute-start.13 = (f32[2,896]{1,0:T(2,128)S(1)}, f32[2,896]{1,0:T(2,128)S(1)}, u32[]{:S(2)}, u32[]{:S(2)}) collective-permute-start(f32[2,896]{1,0:T(2,128)S(1)} %add_add_fusion.11), channel_id=1, source_target_pairs={{0,24},{1,25},{2,26},{3,27},{4,28},{5,29},{6,30},{7,31},{8,16},{9,... | collective-permute-start | bytes 21512 | tf_op jit(solution)/shard_map/ppermute | solution.py:879
  53.6 2.4 collective-permute-done.12
  56.1 4.6 %finish_lower.1 = (bf16[224,896]{1,0:T(8,128)(2,1)S(1)}, f32[224,384]{1,0:T(8,128)S(1)}, f32[224,384]{1,0:T(8,128)S(1)}, f32[3,384]{1,0:T(4,128)S(1)}, f32[2,384]{1,0:T(2,128)S(1)}) custom-call(s32[1]{0:T(128)S(6)} %copy.57.group_ref, s32[3]{0:T(128)S(1)} %copy-done.37, f32[1600,384]{1,0:T(8,128)S(1)} %get-tuple-element.157.zb_ref, ...), custom_call_target="tpu_custom_call" | custom-call | flops 286261248 | bytes 7129616 | tf_op jit(solution)/shard_map/finish_lower/pallas_call | solution.py:39
  62.6 2.4 collective-permute-start.17
  71.3 2.3 collective-permute-start.18
  85.2 2.6 collective-permute-start.27
  96.5 2.5 collective-permute-start.31
  117.1 3.1 conv_backward.2
  130.5 2.5 collective-permute-start.42
  137.6 5.3 %join_blocks.1 = (bf16[224,384]{1,0:T(8,128)(2,1)S(1)}, f32[1600,896]{1,0:T(8,128)S(1)}, f32[2,896]{1,0:T(2,128)S(1)}) custom-call(s32[1]{0:T(128)S(6)} %copy.57.group_ref, s32[3]{0:T(128)S(1)} %copy-done.37, f32[224,384]{1,0:T(8,128)S(1)} %get-tuple-element.186.gua_ref, f32[224,384]{1,0:T(8,128)S(1)} %copy-done.10, f32[3,384]{1,0:T(4,128)S(1)} %add_add_fusion.12.suma_ref, ...), custom_call_target="tpu_custom_call" | custom-call | flops 286261248 | bytes 8000528 | tf_op jit(solution)/shard_map/join_blocks/pallas_call | solution.py:39
  147.6 7.5 %collective-permute-done.46 = f32[2,896]{1,0:T(2,128)S(1)} collective-permute-done((f32[2,896]{1,0:T(2,128)S(1)}, f32[2,896]{1,0:T(2,128)S(1)}, u32[]{:S(2)}, u32[]{:S(2)}) %collective-permute-start.46) | collective-permute-done | bytes 7200 | tf_op jit(solution)/shard_map/ppermute | solution.py:879
  155.1 2.6 collective-permute-start.49
  163.3 3.2 unit_backward.3
  166.5 4.7 %weights.5 = (f32[16,272,128]{2,1,0:T(8,128)S(1)}, f32[16,272,128]{2,1,0:T(8,128)S(1)}) custom-call(s32[1]{0:T(128)} %bitcast.13.me_ref, bf16[1600,1536]{1,0:T(8,128)(2,1)S(1)} %bitcast.93, bf16[1600,1024]{1,0:T(8,128)(2,1)S(1)} %get-tuple-element.221.refs_1_.three_ref, bf16[224,384]{1,0:T(8,128)(2,1)S(1)} %get-tuple-element.207.refs_2_, ...), custom_call_target="tpu_custom_call" | custom-call | flops 3565158400 | bytes 8765444 | tf_op jit(solution)/shard_map/weights/pallas_call | solution.py:39
  171.2 5.4 %collective-permute-done.51 = f32[4,472,128]{2,1,0:T(8,128)S(1)} collective-permute-done((f32[4,472,128]{2,1,0:T(8,128)S(1)}, f32[4,472,128]{2,1,0:T(8,128)S(1)}, u32[]{:S(2)}, u32[]{:S(2)}) %collective-permute-start.51) | collective-permute-done | bytes 966688 | tf_op jit(solution)/shard_map/ppermute | solution.py:947
  176.8 4.3 %collective-permute-done.55 = f32[16,272,128]{2,1,0:T(8,128)S(1)} collective-permute-done((f32[16,272,128]{2,1,0:T(8,128)S(1)}, f32[16,272,128]{2,1,0:T(8,128)S(1)}, u32[]{:S(2)}, u32[]{:S(2)}) %collective-permute-start.55) | collective-permute-done | bytes 2228256 | tf_op jit(solution)/shard_map/ppermute | solution.py:947
  184.2 2.4 collective-permute-start.54
  186.6 13.2 %conv_backward.3 = (f32[1600,384]{1,0:T(8,128)S(1)}, f32[2,384]{1,0:T(2,128)S(1)}) custom-call(s32[1]{0:T(128)S(6)} %copy.57.group_ref, s32[3]{0:T(128)S(1)} %copy-done.37, bf16[1600,1024]{1,0:T(8,128)(2,1)S(1)} %get-tuple-element.221.refs_1_.three_ref, bf16[1600,384]{1,0:T(8,128)(2,1)S(1)} %get-tuple-element.217.thin3_ref.refs_3_, ...), custom_call_target="tpu_custom_call" | custom-call | flops 4423680000 | bytes 10280464 | tf_op jit(solution)/shard_map/conv_backward/pallas_call | solution.py:39
  203.7 5.8 %weights.6 = (f32[16,240,128]{2,1,0:T(8,128)S(1)}, f32[16,240,128]{2,1,0:T(8,128)S(1)}) custom-call(s32[1]{0:T(128)} %bitcast.13.me_ref, bf16[1600,1536]{1,0:T(8,128)(2,1)S(1)} %bitcast.93, bf16[1600,1024]{1,0:T(8,128)(2,1)S(1)} %get-tuple-element.221.refs_1_.three_ref, bf16[1600,384]{1,0:T(8,128)(2,1)S(1)} %copy-done.27, ...), custom_call_target="tpu_custom_call" | custom-call | flops 3145728000 | bytes 14540804 | tf_op jit(solution)/shard_map/weights/pallas_call | solution.py:39
  210.1 3.5 collective-permute-done.63
  219.5 2.5 collective-permute-start.69
  222.0 4.2 %collective-permute-start.68 = (f32[2,384]{1,0:T(2,128)S(1)}, f32[2,384]{1,0:T(2,128)S(1)}, u32[]{:S(2)}, u32[]{:S(2)}) collective-permute-start(f32[2,384]{1,0:T(2,128)S(1)} %add_add_fusion.17), channel_id=1, source_target_pairs={{0,16},{1,17},{2,18},{3,19},{4,20},{5,21},{6,22},{7,23},{8,24},{9,... | collective-permute-start | bytes 9224 | tf_op jit(solution)/shard_map/ppermute | solution.py:879
  233.1 4.3 %last_back.1 = (bf16[1600,384]{1,0:T(8,128)(2,1)S(1)}, bf16[1600,832]{1,0:T(8,128)(2,1)S(1)}) custom-call(s32[1]{0:T(128)S(6)} %copy.57.group_ref, s32[3]{0:T(128)S(1)} %copy-done.37, f32[1600,384]{1,0:T(8,128)S(1)} %get-tuple-element.231.gua_ref, f32[1600,384]{1,0:T(8,128)S(1)} %copy-done.51, f32[3,384]{1,0:T(4,128)S(1)} %add_add_fusion.14.suma_ref.suma1_ref, ...), custom_call_target="tpu_custom_call" | custom-call | flops 2044723200 | bytes 7432720 | tf_op jit(solution)/shard_map/last_back/pallas_call | solution.py:39
  239.0 9.9 %collective-permute-done.57 = f32[472,128]{1,0:T(8,128)S(1)} collective-permute-done((f32[472,128]{1,0:T(8,128)S(1)}, f32[472,128]{1,0:T(8,128)S(1)}, u32[]{:S(2)}, u32[]{:S(2)}) %collective-permute-start.57) | collective-permute-done | bytes 241696 | tf_op jit(solution)/shard_map/ppermute | solution.py:947
  251.2 2.7 copy.36
  255.8 2.5 collective-permute-start.73
  260.4 4.6 %collective-permute-done.71 = f32[272,128]{1,0:T(8,128)S(1)} collective-permute-done((f32[272,128]{1,0:T(8,128)S(1)}, f32[272,128]{1,0:T(8,128)S(1)}, u32[]{:S(2)}, u32[]{:S(2)}) %collective-permute-start.71) | collective-permute-done | bytes 139296 | tf_op jit(solution)/shard_map/ppermute | solution.py:947
  268.6 13.1 %collective-permute-done.77 = f32[4,48,128]{2,1,0:T(8,128)S(1)} collective-permute-done((f32[4,48,128]{2,1,0:T(8,128)S(1)}, f32[4,48,128]{2,1,0:T(8,128)S(1)}, u32[]{:S(2)}, u32[]{:S(2)}) %collective-permute-start.77) | collective-permute-done | bytes 98336 | tf_op jit(solution)/shard_map/ppermute | solution.py:947
  284.8 2.5 collective-permute-start.88
  289.2 2.5 collective-permute-start.85
  293.1 6.5 %collective-permute-done.83 = f32[240,128]{1,0:T(8,128)S(1)} collective-permute-done((f32[240,128]{1,0:T(8,128)S(1)}, f32[240,128]{1,0:T(8,128)S(1)}, u32[]{:S(2)}, u32[]{:S(2)}) %collective-permute-start.83) | collective-permute-done | bytes 122912 | tf_op jit(solution)/shard_map/ppermute | solution.py:947
  302.2 3.3 collective-permute-done.81
  305.5 4.8 %collective-permute-done.80 = f32[272,128]{1,0:T(8,128)S(1)} collective-permute-done((f32[272,128]{1,0:T(8,128)S(1)}, f32[272,128]{1,0:T(8,128)S(1)}, u32[]{:S(2)}, u32[]{:S(2)}) %collective-permute-start.80) | collective-permute-done | bytes 139296 | tf_op jit(solution)/shard_map/ppermute | solution.py:947
  312.2 8.2 %collective-permute-done.90 = f32[4,272,128]{2,1,0:T(8,128)S(1)} collective-permute-done((f32[4,272,128]{2,1,0:T(8,128)S(1)}, f32[4,272,128]{2,1,0:T(8,128)S(1)}, u32[]{:S(2)}, u32[]{:S(2)}) %collective-permute-start.90) | collective-permute-done | bytes 557088 | tf_op jit(solution)/shard_map/ppermute | solution.py:947
  321.4 2.3 collective-permute-start.94
  325.9 4.2 %collective-permute-done.94 = f32[288,128]{1,0:T(8,128)S(1)} collective-permute-done((f32[288,128]{1,0:T(8,128)S(1)}, f32[288,128]{1,0:T(8,128)S(1)}, u32[]{:S(2)}, u32[]{:S(2)}) %collective-permute-start.94) | collective-permute-done | bytes 147488 | tf_op jit(solution)/shard_map/ppermute | solution.py:947
  330.1 5.1 %collective-permute-done.93 = f32[288,128]{1,0:T(8,128)S(1)} collective-permute-done((f32[288,128]{1,0:T(8,128)S(1)}, f32[288,128]{1,0:T(8,128)S(1)}, u32[]{:S(2)}, u32[]{:S(2)}) %collective-permute-start.93) | collective-permute-done | bytes 147488 | tf_op jit(solution)/shard_map/ppermute | solution.py:947
  337.7 8.5 %collective-permute-done.96 = f32[4,288,128]{2,1,0:T(8,128)S(1)} collective-permute-done((f32[4,288,128]{2,1,0:T(8,128)S(1)}, f32[4,288,128]{2,1,0:T(8,128)S(1)}, u32[]{:S(2)}, u32[]{:S(2)}) %collective-permute-start.96) | collective-permute-done | bytes 589856 | tf_op jit(solution)/shard_map/ppermute | solution.py:947
  347.3 3.8 %assemble.3 = (f32[2,832,256]{2,1,0:T(8,128)}, f32[2,160,832]{2,1,0:T(8,128)}, f32[2,27,160,320]{3,2,1,0:T(8,128)}, f32[2,32,832]{2,1,0:T(8,128)}, f32[2,27,32,128]{3,2,1,0:T(8,128)}, /*index=5*/f32[2,832,128]{2,1,0:T(8,128)}) custom-call(s32[1]{0:T(128)} %bitcast.13.me_ref, f32[16,472,128]{2,1,0:T(8,128)S(1)} %pad_maximum_fusion.refs_0_, ...), custom_call_target="tpu_custom_call" | custom-call | bytes 16711680 | tf_op jit(solution)/shard_map/assemble/pallas_call | solution.py:739
  351.1 11.5 %collective-permute-done.97 = f32[8,288,128]{2,1,0:T(8,128)S(1)} collective-permute-done((f32[8,288,128]{2,1,0:T(8,128)S(1)}, f32[8,288,128]{2,1,0:T(8,128)S(1)}, u32[]{:S(2)}, u32[]{:S(2)}) %collective-permute-start.97) | collective-permute-done | bytes 1179680 | tf_op jit(solution)/shard_map/ppermute | solution.py:947
  368.3 2.7 assemble.4
  371.0 4.0 %assemble.5 = (f32[2,832,256]{2,1,0:T(8,128)}, f32[2,160,832]{2,1,0:T(8,128)}, f32[2,27,160,320]{3,2,1,0:T(8,128)}, f32[2,32,832]{2,1,0:T(8,128)}, f32[2,27,32,128]{3,2,1,0:T(8,128)}, /*index=5*/f32[2,832,128]{2,1,0:T(8,128)}) custom-call(s32[1]{0:T(128)} %bitcast.13.me_ref, ...), custom_call_target="tpu_custom_call", output_to_operand_aliasing={{0}: (3, {}), {1}: (4, {}), {2}: (5, {}), {3}: (6, {}), {4}... | custom-call | bytes 9240576 | tf_op jit(solution)/shard_map/assemble/pallas_call | solution.py:739
  (369 shorter events, 149.1 us)
Async XLA Ops:
  16.3 11.7 %collective-permute-start.6 = (f32[3,384]{1,0:T(4,128)S(1)}, f32[3,384]{1,0:T(4,128)S(1)}, u32[]{:S(2)}, u32[]{:S(2)}) collective-permute-start(f32[3,384]{1,0:T(4,128)S(1)} %add_add_fusion.15), channel_id=1, source_target_pairs={{0,24},{1,25},{2,26},{3,27},{4,28},{5,29},{6,30},{7,31},{8,16},{9,... | collective-permute-start | bytes 13832 | tf_op jit(solution)/shard_map/ppermute | solution.py:879
  19.9 8.1 %collective-permute-start.5 = (f32[3,384]{1,0:T(4,128)S(1)}, f32[3,384]{1,0:T(4,128)S(1)}, u32[]{:S(2)}, u32[]{:S(2)}) collective-permute-start(f32[3,384]{1,0:T(4,128)S(1)} %add_add_fusion.15), channel_id=1, source_target_pairs={{0,16},{1,17},{2,18},{3,19},{4,20},{5,21},{6,22},{7,23},{8,24},{9,... | collective-permute-start | bytes 13832 | tf_op jit(solution)/shard_map/ppermute | solution.py:879
  19.9 8.1 %collective-permute-start.4 = (f32[3,384]{1,0:T(4,128)S(1)}, f32[3,384]{1,0:T(4,128)S(1)}, u32[]{:S(2)}, u32[]{:S(2)}) collective-permute-start(f32[3,384]{1,0:T(4,128)S(1)} %add_add_fusion.15), channel_id=1, source_target_pairs={{0,8},{1,9},{2,10},{3,11},{4,12},{5,13},{6,14},{7,15},{8,0},{9,1},... | collective-permute-start | bytes 13832 | tf_op jit(solution)/shard_map/ppermute | solution.py:879
  122.1 6.9 %collective-permute-start.39 = (f32[16,472,128]{2,1,0:T(8,128)S(1)}, f32[16,472,128]{2,1,0:T(8,128)S(1)}, u32[]{:S(2)}, u32[]{:S(2)}) collective-permute-start(f32[16,472,128]{2,1,0:T(8,128)S(1)} %get-tuple-element.196), channel_id=1, source_target_pairs={{0,1},{1,0},{2,3},{3,2},{4,5},{5,4},{6,7},{7,6},{8,9},{9,8},{10,11... | collective-permute-start | bytes 11599880 | tf_op jit(solution)/shard_map/ppermute | solution.py:947
  129.6 32.8 %collective-permute-start.50 = (f32[8,472,128]{2,1,0:T(8,128)S(1)}, f32[8,472,128]{2,1,0:T(8,128)S(1)}, u32[]{:S(2)}, u32[]{:S(2)}) collective-permute-start(f32[8,472,128]{2,1,0:T(8,128)S(1)} %get-tuple-element.200), channel_id=1, source_target_pairs={{0,2},{1,5},{2,0},{3,7},{4,6},{5,1},{6,4},{7,3},{8,10},{9,13},{10,... | collective-permute-start | bytes 5799944 | tf_op jit(solution)/shard_map/ppermute | solution.py:947
  144.1 11.0 %collective-permute-start.46 = (f32[2,896]{1,0:T(2,128)S(1)}, f32[2,896]{1,0:T(2,128)S(1)}, u32[]{:S(2)}, u32[]{:S(2)}) collective-permute-start(f32[2,896]{1,0:T(2,128)S(1)} %add.440), channel_id=1, source_target_pairs={{0,6},{1,7},{2,4},{3,5},{4,2},{5,3},{6,0},{7,1},{8,14},{9,15},{10,... | collective-permute-start | bytes 21512 | tf_op jit(solution)/shard_map/ppermute | solution.py:879
  146.3 8.8 %collective-permute-start.45 = (f32[2,896]{1,0:T(2,128)S(1)}, f32[2,896]{1,0:T(2,128)S(1)}, u32[]{:S(2)}, u32[]{:S(2)}) collective-permute-start(f32[2,896]{1,0:T(2,128)S(1)} %add.440), channel_id=1, source_target_pairs={{0,4},{1,5},{2,6},{3,7},{4,0},{5,1},{6,2},{7,3},{8,12},{9,13},{10,... | collective-permute-start | bytes 21512 | tf_op jit(solution)/shard_map/ppermute | solution.py:879
  146.8 8.3 %collective-permute-start.44 = (f32[2,896]{1,0:T(2,128)S(1)}, f32[2,896]{1,0:T(2,128)S(1)}, u32[]{:S(2)}, u32[]{:S(2)}) collective-permute-start(f32[2,896]{1,0:T(2,128)S(1)} %add.440), channel_id=1, source_target_pairs={{0,2},{1,3},{2,0},{3,1},{4,6},{5,7},{6,4},{7,5},{8,10},{9,11},{10,... | collective-permute-start | bytes 21512 | tf_op jit(solution)/shard_map/ppermute | solution.py:879
  162.6 14.0 %collective-permute-start.51 = (f32[4,472,128]{2,1,0:T(8,128)S(1)}, f32[4,472,128]{2,1,0:T(8,128)S(1)}, u32[]{:S(2)}, u32[]{:S(2)}) collective-permute-start(f32[4,472,128]{2,1,0:T(8,128)S(1)} %get-tuple-element.202), channel_id=1, source_target_pairs={{0,4},{1,3},{2,6},{3,1},{4,0},{5,7},{6,2},{7,5},{8,12},{9,11},{10,... | collective-permute-start | bytes 2899976 | tf_op jit(solution)/shard_map/ppermute | solution.py:947
  181.4 20.2 %collective-permute-start.56 = (f32[8,272,128]{2,1,0:T(8,128)S(1)}, f32[8,272,128]{2,1,0:T(8,128)S(1)}, u32[]{:S(2)}, u32[]{:S(2)}) collective-permute-start(f32[8,272,128]{2,1,0:T(8,128)S(1)} %get-tuple-element.305), channel_id=1, source_target_pairs={{0,2},{1,5},{2,0},{3,7},{4,6},{5,1},{6,4},{7,3},{8,10},{9,13},{10,... | collective-permute-start | bytes 3342344 | tf_op jit(solution)/shard_map/ppermute | solution.py:947
  182.2 19.2 %collective-permute-start.52 = (f32[472,128]{1,0:T(8,128)S(1)}, f32[472,128]{1,0:T(8,128)S(1)}, u32[]{:S(2)}, u32[]{:S(2)}) collective-permute-start(f32[472,128]{1,0:T(8,128)S(1)} %get-tuple-element.211), channel_id=1, source_target_pairs={{0,16},{1,17},{2,18},{3,19},{4,20},{5,21},{6,22},{7,23},{8,24},{9,... | collective-permute-start | bytes 725000 | tf_op jit(solution)/shard_map/ppermute | solution.py:947
  184.2 17.3 %collective-permute-start.53 = (f32[472,128]{1,0:T(8,128)S(1)}, f32[472,128]{1,0:T(8,128)S(1)}, u32[]{:S(2)}, u32[]{:S(2)}) collective-permute-start(f32[472,128]{1,0:T(8,128)S(1)} %get-tuple-element.212), channel_id=1, source_target_pairs={{0,8},{1,9},{2,10},{3,11},{4,12},{5,13},{6,14},{7,15},{8,0},{9,1},... | collective-permute-start | bytes 725000 | tf_op jit(solution)/shard_map/ppermute | solution.py:947
  184.2 17.3 %collective-permute-start.54 = (f32[472,128]{1,0:T(8,128)S(1)}, f32[472,128]{1,0:T(8,128)S(1)}, u32[]{:S(2)}, u32[]{:S(2)}) collective-permute-start(f32[472,128]{1,0:T(8,128)S(1)} %get-tuple-element.213), channel_id=1, source_target_pairs={{0,24},{1,25},{2,26},{3,27},{4,28},{5,29},{6,30},{7,31},{8,16},{9,... | collective-permute-start | bytes 725000 | tf_op jit(solution)/shard_map/ppermute | solution.py:947
  209.5 7.6 %collective-permute-start.61 = (f32[16,240,128]{2,1,0:T(8,128)S(1)}, f32[16,240,128]{2,1,0:T(8,128)S(1)}, u32[]{:S(2)}, u32[]{:S(2)}) collective-permute-start(f32[16,240,128]{2,1,0:T(8,128)S(1)} %get-tuple-element.230), channel_id=1, source_target_pairs={{0,1},{1,0},{2,3},{3,2},{4,5},{5,4},{6,7},{7,6},{8,9},{9,8},{10,11... | collective-permute-start | bytes 5898248 | tf_op jit(solution)/shard_map/ppermute | solution.py:947
  217.3 31.8 %collective-permute-start.62 = (f32[8,240,128]{2,1,0:T(8,128)S(1)}, f32[8,240,128]{2,1,0:T(8,128)S(1)}, u32[]{:S(2)}, u32[]{:S(2)}) collective-permute-start(f32[8,240,128]{2,1,0:T(8,128)S(1)} %get-tuple-element.307), channel_id=1, source_target_pairs={{0,2},{1,5},{2,0},{3,7},{4,6},{5,1},{6,4},{7,3},{8,10},{9,13},{10,... | collective-permute-start | bytes 2949128 | tf_op jit(solution)/shard_map/ppermute | solution.py:947
  219.5 8.2 %collective-permute-start.69 = (f32[2,384]{1,0:T(2,128)S(1)}, f32[2,384]{1,0:T(2,128)S(1)}, u32[]{:S(2)}, u32[]{:S(2)}) collective-permute-start(f32[2,384]{1,0:T(2,128)S(1)} %add_add_fusion.17), channel_id=1, source_target_pairs={{0,24},{1,25},{2,26},{3,27},{4,28},{5,29},{6,30},{7,31},{8,16},{9,... | collective-permute-start | bytes 9224 | tf_op jit(solution)/shard_map/ppermute | solution.py:879
  222.0 6.7 %collective-permute-start.68 = (f32[2,384]{1,0:T(2,128)S(1)}, f32[2,384]{1,0:T(2,128)S(1)}, u32[]{:S(2)}, u32[]{:S(2)}) collective-permute-start(f32[2,384]{1,0:T(2,128)S(1)} %add_add_fusion.17), channel_id=1, source_target_pairs={{0,16},{1,17},{2,18},{3,19},{4,20},{5,21},{6,22},{7,23},{8,24},{9,... | collective-permute-start | bytes 9224 | tf_op jit(solution)/shard_map/ppermute | solution.py:879
  226.2 12.8 %collective-permute-start.59 = (f32[472,128]{1,0:T(8,128)S(1)}, f32[472,128]{1,0:T(8,128)S(1)}, u32[]{:S(2)}, u32[]{:S(2)}) collective-permute-start(f32[472,128]{1,0:T(8,128)S(1)} %add_add_fusion), channel_id=1, source_target_pairs={{0,24},{1,25},{2,26},{3,27},{4,28},{5,29},{6,30},{7,31},{8,16},{9,... | collective-permute-start | bytes 725000 | tf_op jit(solution)/shard_map/ppermute | solution.py:947
  227.7 11.3 %collective-permute-start.58 = (f32[472,128]{1,0:T(8,128)S(1)}, f32[472,128]{1,0:T(8,128)S(1)}, u32[]{:S(2)}, u32[]{:S(2)}) collective-permute-start(f32[472,128]{1,0:T(8,128)S(1)} %add_add_fusion), channel_id=1, source_target_pairs={{0,8},{1,9},{2,10},{3,11},{4,12},{5,13},{6,14},{7,15},{8,0},{9,1},... | collective-permute-start | bytes 725000 | tf_op jit(solution)/shard_map/ppermute | solution.py:947
  228.7 20.2 %collective-permute-start.57 = (f32[472,128]{1,0:T(8,128)S(1)}, f32[472,128]{1,0:T(8,128)S(1)}, u32[]{:S(2)}, u32[]{:S(2)}) collective-permute-start(f32[472,128]{1,0:T(8,128)S(1)} %add_add_fusion), channel_id=1, source_target_pairs={{0,16},{1,17},{2,18},{3,19},{4,20},{5,21},{6,22},{7,23},{8,24},{9,... | collective-permute-start | bytes 725000 | tf_op jit(solution)/shard_map/ppermute | solution.py:947
  231.7 17.3 %collective-permute-start.60 = (f32[4,272,128]{2,1,0:T(8,128)S(1)}, f32[4,272,128]{2,1,0:T(8,128)S(1)}, u32[]{:S(2)}, u32[]{:S(2)}) collective-permute-start(f32[4,272,128]{2,1,0:T(8,128)S(1)} %get-tuple-element.228), channel_id=1, source_target_pairs={{0,4},{1,3},{2,6},{3,1},{4,0},{5,7},{6,2},{7,5},{8,12},{9,11},{10,... | collective-permute-start | bytes 1671176 | tf_op jit(solution)/shard_map/ppermute | solution.py:947
  249.2 10.4 %collective-permute-start.75 = (f32[16,48,128]{2,1,0:T(8,128)S(1)}, f32[16,48,128]{2,1,0:T(8,128)S(1)}, u32[]{:S(2)}, u32[]{:S(2)}) collective-permute-start(f32[16,48,128]{2,1,0:T(8,128)S(1)} %get-tuple-element.244), channel_id=1, source_target_pairs={{0,1},{1,0},{2,3},{3,2},{4,5},{5,4},{6,7},{7,6},{8,9},{9,8},{10,11... | collective-permute-start | bytes 1179656 | tf_op jit(solution)/shard_map/ppermute | solution.py:947
  253.9 11.1 %collective-permute-start.71 = (f32[272,128]{1,0:T(8,128)S(1)}, f32[272,128]{1,0:T(8,128)S(1)}, u32[]{:S(2)}, u32[]{:S(2)}) collective-permute-start(f32[272,128]{1,0:T(8,128)S(1)} %get-tuple-element.238), channel_id=1, source_target_pairs={{0,16},{1,17},{2,18},{3,19},{4,20},{5,21},{6,22},{7,23},{8,24},{9,... | collective-permute-start | bytes 417800 | tf_op jit(solution)/shard_map/ppermute | solution.py:947
  253.9 12.5 %collective-permute-start.72 = (f32[272,128]{1,0:T(8,128)S(1)}, f32[272,128]{1,0:T(8,128)S(1)}, u32[]{:S(2)}, u32[]{:S(2)}) collective-permute-start(f32[272,128]{1,0:T(8,128)S(1)} %get-tuple-element.239), channel_id=1, source_target_pairs={{0,8},{1,9},{2,10},{3,11},{4,12},{5,13},{6,14},{7,15},{8,0},{9,1},... | collective-permute-start | bytes 417800 | tf_op jit(solution)/shard_map/ppermute | solution.py:947
  255.8 11.8 %collective-permute-start.73 = (f32[272,128]{1,0:T(8,128)S(1)}, f32[272,128]{1,0:T(8,128)S(1)}, u32[]{:S(2)}, u32[]{:S(2)}) collective-permute-start(f32[272,128]{1,0:T(8,128)S(1)} %get-tuple-element.240), channel_id=1, source_target_pairs={{0,24},{1,25},{2,26},{3,27},{4,28},{5,29},{6,30},{7,31},{8,16},{9,... | collective-permute-start | bytes 417800 | tf_op jit(solution)/shard_map/ppermute | solution.py:947
  258.3 23.4 %collective-permute-start.74 = (f32[4,240,128]{2,1,0:T(8,128)S(1)}, f32[4,240,128]{2,1,0:T(8,128)S(1)}, u32[]{:S(2)}, u32[]{:S(2)}) collective-permute-start(f32[4,240,128]{2,1,0:T(8,128)S(1)} %get-tuple-element.242), channel_id=1, source_target_pairs={{0,4},{1,3},{2,6},{3,1},{4,0},{5,7},{6,2},{7,5},{8,12},{9,11},{10,... | collective-permute-start | bytes 1474568 | tf_op jit(solution)/shard_map/ppermute | solution.py:947
  259.6 22.1 %collective-permute-start.70 = (f32[4,472,128]{2,1,0:T(8,128)S(1)}, f32[4,472,128]{2,1,0:T(8,128)S(1)}, u32[]{:S(2)}, u32[]{:S(2)}) collective-permute-start(f32[4,472,128]{2,1,0:T(8,128)S(1)} %pad_maximum_fusion.6), channel_id=1, source_target_pairs={{0,4},{1,3},{2,6},{3,1},{4,0},{5,7},{6,2},{7,5},{8,12},{9,11},{10,... | collective-permute-start | bytes 2899976 | tf_op jit(solution)/shard_map/ppermute | solution.py:947
  265.0 16.7 %collective-permute-start.77 = (f32[4,48,128]{2,1,0:T(8,128)S(1)}, f32[4,48,128]{2,1,0:T(8,128)S(1)}, u32[]{:S(2)}, u32[]{:S(2)}) collective-permute-start(f32[4,48,128]{2,1,0:T(8,128)S(1)} %slice.395), channel_id=1, source_target_pairs={{0,4},{1,3},{2,6},{3,1},{4,0},{5,7},{6,2},{7,5},{8,12},{9,11},{10,... | collective-permute-start | bytes 294920 | tf_op jit(solution)/shard_map/ppermute | solution.py:947
  266.4 15.3 %collective-permute-start.76 = (f32[4,48,128]{2,1,0:T(8,128)S(1)}, f32[4,48,128]{2,1,0:T(8,128)S(1)}, u32[]{:S(2)}, u32[]{:S(2)}) collective-permute-start(f32[4,48,128]{2,1,0:T(8,128)S(1)} %get-tuple-element.332), channel_id=1, source_target_pairs={{0,2},{1,5},{2,0},{3,7},{4,6},{5,1},{6,4},{7,3},{8,10},{9,13},{10,... | collective-permute-start | bytes 294920 | tf_op jit(solution)/shard_map/ppermute | solution.py:947
  267.6 14.1 %collective-permute-start.78 = (f32[4,48,128]{2,1,0:T(8,128)S(1)}, f32[4,48,128]{2,1,0:T(8,128)S(1)}, u32[]{:S(2)}, u32[]{:S(2)}) collective-permute-start(f32[4,48,128]{2,1,0:T(8,128)S(1)} %get-tuple-element.333), channel_id=1, source_target_pairs={{0,6},{1,7},{2,4},{3,5},{4,2},{5,3},{6,0},{7,1},{8,14},{9,15},{10,... | collective-permute-start | bytes 294920 | tf_op jit(solution)/shard_map/ppermute | solution.py:947
  281.9 28.5 %collective-permute-start.79 = (f32[8,472,128]{2,1,0:T(8,128)S(1)}, f32[8,472,128]{2,1,0:T(8,128)S(1)}, u32[]{:S(2)}, u32[]{:S(2)}) collective-permute-start(f32[8,472,128]{2,1,0:T(8,128)S(1)} %pad_maximum_fusion.3), channel_id=1, source_target_pairs={{0,2},{1,5},{2,0},{3,7},{4,6},{5,1},{6,4},{7,3},{8,10},{9,13},{10,... | collective-permute-start | bytes 5799944 | tf_op jit(solution)/shard_map/ppermute | solution.py:947
  282.9 6.3 %collective-permute-start.87 = (f32[48,128]{1,0:T(8,128)S(1)}, f32[48,128]{1,0:T(8,128)S(1)}, u32[]{:S(2)}, u32[]{:S(2)}) collective-permute-start(f32[48,128]{1,0:T(8,128)S(1)} %get-tuple-element.257), channel_id=1, source_target_pairs={{0,8},{1,9},{2,10},{3,11},{4,12},{5,13},{6,14},{7,15},{8,0},{9,1},... | collective-permute-start | bytes 73736 | tf_op jit(solution)/shard_map/ppermute | solution.py:947
  284.8 6.9 %collective-permute-start.88 = (f32[48,128]{1,0:T(8,128)S(1)}, f32[48,128]{1,0:T(8,128)S(1)}, u32[]{:S(2)}, u32[]{:S(2)}) collective-permute-start(f32[48,128]{1,0:T(8,128)S(1)} %get-tuple-element.258), channel_id=1, source_target_pairs={{0,24},{1,25},{2,26},{3,27},{4,28},{5,29},{6,30},{7,31},{8,16},{9,... | collective-permute-start | bytes 73736 | tf_op jit(solution)/shard_map/ppermute | solution.py:947
  287.3 12.3 %collective-permute-start.83 = (f32[240,128]{1,0:T(8,128)S(1)}, f32[240,128]{1,0:T(8,128)S(1)}, u32[]{:S(2)}, u32[]{:S(2)}) collective-permute-start(f32[240,128]{1,0:T(8,128)S(1)} %get-tuple-element.252), channel_id=1, source_target_pairs={{0,16},{1,17},{2,18},{3,19},{4,20},{5,21},{6,22},{7,23},{8,24},{9,... | collective-permute-start | bytes 368648 | tf_op jit(solution)/shard_map/ppermute | solution.py:947
  289.0 11.7 %collective-permute-start.84 = (f32[240,128]{1,0:T(8,128)S(1)}, f32[240,128]{1,0:T(8,128)S(1)}, u32[]{:S(2)}, u32[]{:S(2)}) collective-permute-start(f32[240,128]{1,0:T(8,128)S(1)} %get-tuple-element.253), channel_id=1, source_target_pairs={{0,8},{1,9},{2,10},{3,11},{4,12},{5,13},{6,14},{7,15},{8,0},{9,1},... | collective-permute-start | bytes 368648 | tf_op jit(solution)/shard_map/ppermute | solution.py:947
  289.2 13.0 %collective-permute-start.85 = (f32[240,128]{1,0:T(8,128)S(1)}, f32[240,128]{1,0:T(8,128)S(1)}, u32[]{:S(2)}, u32[]{:S(2)}) collective-permute-start(f32[240,128]{1,0:T(8,128)S(1)} %get-tuple-element.254), channel_id=1, source_target_pairs={{0,24},{1,25},{2,26},{3,27},{4,28},{5,29},{6,30},{7,31},{8,16},{9,... | collective-permute-start | bytes 368648 | tf_op jit(solution)/shard_map/ppermute | solution.py:947
  291.7 10.6 %collective-permute-start.82 = (f32[272,128]{1,0:T(8,128)S(1)}, f32[272,128]{1,0:T(8,128)S(1)}, u32[]{:S(2)}, u32[]{:S(2)}) collective-permute-start(f32[272,128]{1,0:T(8,128)S(1)} %add_add_fusion.1), channel_id=1, source_target_pairs={{0,24},{1,25},{2,26},{3,27},{4,28},{5,29},{6,30},{7,31},{8,16},{9,... | collective-permute-start | bytes 417800 | tf_op jit(solution)/shard_map/ppermute | solution.py:947
  300.6 9.7 %collective-permute-start.80 = (f32[272,128]{1,0:T(8,128)S(1)}, f32[272,128]{1,0:T(8,128)S(1)}, u32[]{:S(2)}, u32[]{:S(2)}) collective-permute-start(f32[272,128]{1,0:T(8,128)S(1)} %add_add_fusion.1), channel_id=1, source_target_pairs={{0,16},{1,17},{2,18},{3,19},{4,20},{5,21},{6,22},{7,23},{8,24},{9,... | collective-permute-start | bytes 417800 | tf_op jit(solution)/shard_map/ppermute | solution.py:947
  310.7 25.5 %collective-permute-start.89 = (f32[16,472,128]{2,1,0:T(8,128)S(1)}, f32[16,472,128]{2,1,0:T(8,128)S(1)}, u32[]{:S(2)}, u32[]{:S(2)}) collective-permute-start(f32[16,472,128]{2,1,0:T(8,128)S(1)} %pad_maximum_fusion.refs_0_), channel_id=1, source_target_pairs={{0,1},{1,0},{2,3},{3,2},{4,5},{5,4},{6,7},{7,6},{8,9},{9,8},{10,11... | collective-permute-start | bytes 11599880 | tf_op jit(solution)/shard_map/ppermute | solution.py:947
  310.7 9.6 %collective-permute-start.90 = (f32[4,272,128]{2,1,0:T(8,128)S(1)}, f32[4,272,128]{2,1,0:T(8,128)S(1)}, u32[]{:S(2)}, u32[]{:S(2)}) collective-permute-start(f32[4,272,128]{2,1,0:T(8,128)S(1)} %pad_maximum_fusion.8), channel_id=1, source_target_pairs={{0,4},{1,3},{2,6},{3,1},{4,0},{5,7},{6,2},{7,5},{8,12},{9,11},{10,... | collective-permute-start | bytes 1671176 | tf_op jit(solution)/shard_map/ppermute | solution.py:947
  320.4 15.6 %collective-permute-start.91 = (f32[8,272,128]{2,1,0:T(8,128)S(1)}, f32[8,272,128]{2,1,0:T(8,128)S(1)}, u32[]{:S(2)}, u32[]{:S(2)}) collective-permute-start(f32[8,272,128]{2,1,0:T(8,128)S(1)} %pad_maximum_fusion.5), channel_id=1, source_target_pairs={{0,2},{1,5},{2,0},{3,7},{4,6},{5,1},{6,4},{7,3},{8,10},{9,13},{10,... | collective-permute-start | bytes 3342344 | tf_op jit(solution)/shard_map/ppermute | solution.py:947
  321.4 8.7 %collective-permute-start.94 = (f32[288,128]{1,0:T(8,128)S(1)}, f32[288,128]{1,0:T(8,128)S(1)}, u32[]{:S(2)}, u32[]{:S(2)}) collective-permute-start(f32[288,128]{1,0:T(8,128)S(1)} %constant_dynamic-update-slice_fusion), channel_id=1, source_target_pairs={{0,24},{1,25},{2,26},{3,27},{4,28},{5,29},{6,30},{7,31},{8,16},{9,... | collective-permute-start | bytes 442376 | tf_op jit(solution)/shard_map/ppermute | solution.py:947
  323.7 11.4 %collective-permute-start.93 = (f32[288,128]{1,0:T(8,128)S(1)}, f32[288,128]{1,0:T(8,128)S(1)}, u32[]{:S(2)}, u32[]{:S(2)}) collective-permute-start(f32[288,128]{1,0:T(8,128)S(1)} %constant_dynamic-update-slice_fusion), channel_id=1, source_target_pairs={{0,8},{1,9},{2,10},{3,11},{4,12},{5,13},{6,14},{7,15},{8,0},{9,1},... | collective-permute-start | bytes 442376 | tf_op jit(solution)/shard_map/ppermute | solution.py:947
  323.7 11.6 %collective-permute-start.92 = (f32[288,128]{1,0:T(8,128)S(1)}, f32[288,128]{1,0:T(8,128)S(1)}, u32[]{:S(2)}, u32[]{:S(2)}) collective-permute-start(f32[288,128]{1,0:T(8,128)S(1)} %constant_dynamic-update-slice_fusion), channel_id=1, source_target_pairs={{0,16},{1,17},{2,18},{3,19},{4,20},{5,21},{6,22},{7,23},{8,24},{9,... | collective-permute-start | bytes 442376 | tf_op jit(solution)/shard_map/ppermute | solution.py:947
  336.2 26.5 %collective-permute-start.95 = (f32[16,272,128]{2,1,0:T(8,128)S(1)}, f32[16,272,128]{2,1,0:T(8,128)S(1)}, u32[]{:S(2)}, u32[]{:S(2)}) collective-permute-start(f32[16,272,128]{2,1,0:T(8,128)S(1)} %pad_maximum_fusion.2.refs_0_), channel_id=1, source_target_pairs={{0,1},{1,0},{2,3},{3,2},{4,5},{5,4},{6,7},{7,6},{8,9},{9,8},{10,11... | collective-permute-start | bytes 6684680 | tf_op jit(solution)/shard_map/ppermute | solution.py:947
  336.2 9.9 %collective-permute-start.96 = (f32[4,288,128]{2,1,0:T(8,128)S(1)}, f32[4,288,128]{2,1,0:T(8,128)S(1)}, u32[]{:S(2)}, u32[]{:S(2)}) collective-permute-start(f32[4,288,128]{2,1,0:T(8,128)S(1)} %pad_maximum_fusion.7), channel_id=1, source_target_pairs={{0,4},{1,3},{2,6},{3,1},{4,0},{5,7},{6,2},{7,5},{8,12},{9,11},{10,... | collective-permute-start | bytes 1769480 | tf_op jit(solution)/shard_map/ppermute | solution.py:947
  346.3 16.3 %collective-permute-start.97 = (f32[8,288,128]{2,1,0:T(8,128)S(1)}, f32[8,288,128]{2,1,0:T(8,128)S(1)}, u32[]{:S(2)}, u32[]{:S(2)}) collective-permute-start(f32[8,288,128]{2,1,0:T(8,128)S(1)} %pad_maximum_fusion.4), channel_id=1, source_target_pairs={{0,2},{1,5},{2,0},{3,7},{4,6},{5,1},{6,4},{7,3},{8,10},{9,13},{10,... | collective-permute-start | bytes 3538952 | tf_op jit(solution)/shard_map/ppermute | solution.py:947
  364.2 6.9 %collective-permute-start.98 = (f32[16,288,128]{2,1,0:T(8,128)S(1)}, f32[16,288,128]{2,1,0:T(8,128)}, u32[]{:S(2)}, u32[]{:S(2)}) collective-permute-start(f32[16,288,128]{2,1,0:T(8,128)S(1)} %pad_maximum_fusion.1.refs_0_), channel_id=1, source_target_pairs={{0,1},{1,0},{2,3},{3,2},{4,5},{5,4},{6,7},{7,6},{8,9},{9,8},{10,11... | collective-permute-start | bytes 7077896 | tf_op jit(solution)/shard_map/ppermute | solution.py:947
  (108 other events, 673.2 us)
where the time goes:
time: 379 us; the launch traced here: 375 us
  waiting for transfers between devices  143 us (38%)
  starting transfers between devices  113 us (30%)
  Pallas kernels  84.4 us (22%)
  local copies, waits for them, and re-layouts  29.5 us (8%)
    ppermute x43, waiting for transfers between devices, swap(): lax.ppermute(value, AXES, [(i, i ^ masks[i & 1]) for i in range(self.tota...  95.1 us
    pallas_call x16, Pallas kernels, call(): pl.pallas_call(body, out_shape=tuple(outs), in_specs=[SMEM] * scalars + [...  68.1 us
    ppermute x56, starting transfers between devices, swap(): return lax.ppermute(value, AXES, [(i, i ^ mask) for i in range(total)])  67.7 us
    ppermute x56, waiting for transfers between devices, swap(): return lax.ppermute(value, AXES, [(i, i ^ mask) for i in range(total)])  47.6 us
    ppermute x43, starting transfers between devices, swap(): lax.ppermute(value, AXES, [(i, i ^ masks[i & 1]) for i in range(self.tota...  45 us
    unnamed x116, local copies, waits for them, and re-layouts  22.9 us
    pallas_call x3, Pallas kernels, assemble_call(): pl.pallas_call(functools.partial(assemble, [(part, len(found) == 2) for p...  10.5 us
  transfers between devices with their start and end apart: 99, of which 61 were waited for; matrix products, arithmetic and copies ran while one was open for 2% of the time, Pallas kernels for 13%

commit v1 on v0

--- a/solution.py
+++ b/solution.py
@@ -35,19 +35,47 @@
     return total + room * MIB
 
 
-def call(body, ins, outs, scratch=(), scalars=2, room=8, flops=0, name=None):
+def with_fetch(body, scalars, fetch, late, many_ins, many_outs, *refs):
+    ins, outs = list(refs[0:many_ins]), refs[many_ins : many_ins + many_outs]
+    scratch = list(refs[many_ins + many_outs :])
+    sems = scratch.pop()
+    moved = fetch + late
+    parts = scratch[len(scratch) - len(moved) :]
+    scratch = scratch[0 : len(scratch) - len(moved)]
+    copies = [pltpu.make_async_copy(ins[i], part, sems.at[k]) for k, (i, part) in enumerate(zip(moved, parts))]
+    for copy in copies:
+        copy.start()
+    for copy in copies[0 : len(fetch)]:
+        copy.wait()
+    for i, part in zip(moved, parts):
+        ins[i] = part
+
+    def ready():
+        for copy in copies[len(fetch) :]:
+            copy.wait()
+
+    body(*ins, *outs, *scratch, **({"ready": ready} if late else {}))
+
+
+def call(body, ins, outs, scratch=(), scalars=2, room=3, name=None, fetch=(), late=()):
+    fetch, late, scratch = list(fetch), list(late), list(scratch)
+    specs = [SMEM] * scalars + [VMEM] * (len(ins) - scalars)
+    if fetch or late:
+        body = functools.partial(with_fetch, body, scalars, fetch, late, len(ins), len(outs))
+        for i in fetch + late:
+            specs[i] = pl.BlockSpec(memory_space=pl.ANY)
+            scratch.append(pltpu.VMEM(ins[i].shape, ins[i].dtype))
+    limit = scoped(scratch, room)
+    if fetch or late:
+        scratch.append(pltpu.SemaphoreType.DMA((len(fetch) + len(late),)))
     return pl.pallas_call(
         body,
         out_shape=tuple(outs),
-        in_specs=[SMEM] * scalars + [VMEM] * (len(ins) - scalars),
+        in_specs=specs,
         out_specs=tuple([VMEM] * len(outs)),
-        scratch_shapes=list(scratch),
-        compiler_params=pltpu.CompilerParams(vmem_limit_bytes=scoped(scratch, room)),
-        cost_estimate=pl.CostEstimate(
-            flops=flops,
-            bytes_accessed=sum(x.size * x.dtype.itemsize for x in ins),
-            transcendentals=0,
-        ),
+        scratch_shapes=scratch,
+        compiler_params=pltpu.CompilerParams(vmem_limit_bytes=limit),
+        cost_estimate=pl.CostEstimate(flops=1, bytes_accessed=1, transcendentals=0),
         name=name,
     )(*ins)
 
@@ -398,9 +426,27 @@
         thin3_ref[rows, tile(k)] = empty
 
 
+def unit_and_weights(
+    layer, parts, columns, group_ref, sides_ref, me_ref, gu_ref, zb_ref, zc_ref, suma_ref, sums_ref, back_ref, par_ref,
+    wide_ref, dza_ref, q_ref, thin_ref, x_ref, dzb_ref, three_ref, thin3_ref, keep_ref, send_ref, other_keep_ref,
+    other_send_ref, around, flat, wide_grad, last_grad, other_wide_grad, thin_grad, point_grad,
+):
+    unit_backward(
+        layer, group_ref, sides_ref, gu_ref, zb_ref, zc_ref, suma_ref, sums_ref, back_ref, par_ref,
+        dzb_ref, three_ref, thin3_ref, around, flat,
+    )
+    weights(
+        parts[0], columns[0], "wl", me_ref, wide_ref, three_ref, dza_ref, q_ref, keep_ref, send_ref, wide_grad, last_grad
+    )
+    weights(
+        parts[1], columns[1], "wo", me_ref, wide_ref, three_ref, thin_ref, thin3_ref, x_ref, dzb_ref, other_keep_ref,
+        other_send_ref, other_wide_grad, thin_grad, point_grad,
+    )
+
+
 def conv_backward(
     layer, group_ref, sides_ref, three_ref, thin3_ref, za_ref, suma_ref, para_ref, wt_ref, wnt_ref,
-    gua_ref, backa_ref, around, shifts, thins, rem, main,
+    gua_ref, backa_ref, around, shifts, thins, rem, main, ready=lambda: None,
 ):
     frames, frame, side = layer.frames, layer.frame, layer.side
     mask = crop_mask(frame, side, crop_of(group_ref, sides_ref, layer.halved))
@@ -438,6 +484,8 @@
                     mixed[k // 2] = shifted if held is None else held + shifted
         for g in range(5):
             shifts[:, tile(18 + g)] = mixed[g].astype(LOW)
+        if t == 0:
+            ready()
         product = dot_nt(shifts[...], wt_ref[...])
         thin = dot_nt(thins[...], wnt_ref[...])
         for k in range(3):
@@ -580,12 +628,6 @@
     segments(wide(0, 4, 5, 7) + point_and_thin(0)),
     segments(last(0)),
 ]
-
-
-def joined_part(first, second):
-    rows = first[0]
-    pieces = [a + [(name, low, end, row + rows) for name, low, end, row in b] for a, b in zip(first[1], second[1])]
-    return rows + second[0], pieces
 
 
 def piece_value(piece, rows, read):
@@ -743,10 +785,8 @@
         out_specs=tuple([anywhere] * 6),
         scratch_shapes=scratch + [pltpu.SemaphoreType.DMA((len(targets),))],
         input_output_aliases={} if outs is None else {1 + len(arrays) + i: i for i in range(6)},
-        compiler_params=pltpu.CompilerParams(vmem_limit_bytes=scoped(scratch, 8)),
-        cost_estimate=pl.CostEstimate(
-            flops=0, bytes_accessed=2 * scoped(scratch, 0), transcendentals=0
-        ),
+        compiler_params=pltpu.CompilerParams(vmem_limit_bytes=scoped(scratch, 3)),
+        cost_estimate=pl.CostEstimate(flops=1, bytes_accessed=1, transcendentals=0),
         name="assemble",
     )(me, *arrays, *([] if outs is None else outs))
 
@@ -865,9 +905,7 @@
         out_specs=tuple([VMEM] * len(outs)),
         scratch_shapes=scratch + [pltpu.SemaphoreType.DMA((len(split),))],
         compiler_params=pltpu.CompilerParams(vmem_limit_bytes=scoped(scratch, 4)),
-        cost_estimate=pl.CostEstimate(
-            flops=0, bytes_accessed=2 * sum(x.size * x.dtype.itemsize for x in outs), transcendentals=0
-        ),
+        cost_estimate=pl.CostEstimate(flops=1, bytes_accessed=1, transcendentals=0),
         name=name,
     )(*whole, *split)
 
@@ -912,10 +950,9 @@
 
 
 def meet(*holders):
-    names = ("value",), ("keep", "send"), ("array",)
-    found = [next(n for n in names if hasattr(holder, n[0])) for holder in holders]
-    values = lax.optimization_barrier([[getattr(h, n) for n in ns] for h, ns in zip(holders, found)])
-    for holder, ns, got in zip(holders, found, values):
+    names = [[n for n in ("value", "keep", "send", "ready", "array") if getattr(holder, n, None) is not None] for holder in holders]
+    values = lax.optimization_barrier([[getattr(h, n) for n in ns] for h, ns in zip(holders, names)])
+    for holder, ns, got in zip(holders, names, values):
         for n, value in zip(ns, got):
             setattr(holder, n, value)
 
@@ -950,60 +987,92 @@
         return Chain(self, keep, send)
 
 
+CORE, FIRST, SECOND, BOTH = ((0,), (0,)), ((1,), (2,)), ((2,), (1,)), ((1, 2), (1, 2))
+FAR, NEAR, ENDS = ((4,), (4,)), ((3,), (3,)), ((3, 4), (3, 4))
+
+
 class Chain:
     def __init__(self, sharing, keep, send, short=False):
-        self.sharing, self.keep, self.send, self.stage = sharing, keep, send, 0
-        self.short = short
+        self.sharing, self.keep, self.send, self.short = sharing, keep, send, short
+        self.ready = None
+        names = ["core", "both" if short else "first", None if short else "second", "depth"]
+        self.stages = [n for n in names + ["up_depth"] + ["up_" + n for n in reversed(names[0:3]) if n] if n]
         if not sharing.able:
-            self.keep, self.send = lax.psum(keep, AXES), lax.psum(send, AXES)
-
-    def step(self):
-        if not self.sharing.able:
-            return
-        swap = self.sharing.swap
-        send = self.send
-        if self.short and self.stage == 1:
-            kept = self.keep
-            got = [swap(send[0:4], (1,), (2,)), swap(kept[4:8], (2,), (1,)), swap(send[4:8], (1, 2))]
-            parts = [(kept[i] + got[0][i]) + (got[1][i] + got[2][i]) for i in range(4)]
-            self.keep, self.send = parts[0], parts[1:]
-            self.stage += 1
-        elif self.short and self.stage == 5:
-            self.send = jnp.concatenate([send, swap(send, (2,), (1,)), swap(send, (1,), (2,)), swap(send, (1, 2))])
-            self.stage += 1
-        elif self.stage < 3:
-            got = swap(send, *(((0,),), ((1,), (2,)), ((2,), (1,)))[self.stage])
-            half = 8 >> self.stage
-            if self.stage < 2:
-                self.keep, self.send = self.keep[0:half] + got[0:half], self.keep[half:] + got[half:]
-            else:
-                parts = [self.keep[i] + got[i] for i in range(4)]
-                self.keep, self.send = parts[0], parts[1:]
-        elif self.stage == 3:
-            got = [swap(send[0], (4,)), swap(send[1], (3,)), swap(send[2], (3, 4))]
-            whole = (self.keep + got[0]) + (got[1] + got[2])
+            self.keep, self.send, self.stages = lax.psum(keep, AXES), lax.psum(send, AXES), []
+
+    def offers(self):
+        stage, send, keep = self.stages[0], self.send, self.keep
+        if stage in ("core", "up_core"):
+            return [(CORE, send)]
+        if stage in ("first", "up_first"):
+            return [(FIRST, send)]
+        if stage in ("second", "up_second"):
+            return [(SECOND, send)]
+        if stage == "both":
+            return [(FIRST, send[0:4]), (SECOND, keep[4:8]), (BOTH, send[4:8])]
+        if stage == "up_both":
+            return [(SECOND, send), (FIRST, send), (BOTH, send)]
+        if stage == "depth":
+            return [(FAR, send[0]), (NEAR, send[1]), (ENDS, send[2])]
+        return [(FAR, send), (NEAR, send), (ENDS, send)]
+
+    def accept(self, got):
+        stage, send, keep = self.stages.pop(0), self.send, self.keep
+        if stage in ("core", "first"):
+            half = keep.shape[0] // 2
+            self.keep, self.send = keep[0:half] + got[0][0:half], keep[half:] + got[0][half:]
+        elif stage == "second":
+            self.split([keep[i] + got[0][i] for i in range(4)])
+        elif stage == "both":
+            self.split([(keep[i] + got[0][i]) + (got[1][i] + got[2][i]) for i in range(4)])
+        elif stage == "depth":
+            whole = (keep + got[0]) + (got[1] + got[2])
             for bit in self.sharing.other:
                 whole = exchange(whole, self.sharing.sizes, [bit])
-            self.send = whole
-            self.keep = ()
-            self.whole = True
-        elif self.stage == 4:
-            self.send = jnp.stack([send, swap(send, (4,)), swap(send, (3,)), swap(send, (3, 4))])
-        elif self.stage < 7:
-            self.send = jnp.concatenate([send, swap(send, *(((2,), (1,)), ((1,), (2,)))[self.stage - 5])])
+            self.keep, self.send = None, whole
+        elif stage == "up_depth":
+            self.send = jnp.stack([send, *got])
+        elif stage == "up_core":
+            self.keep, self.send = send, got[0]
         else:
-            self.keep, self.send = send, swap(send, (0,))
-        self.stage += 1
-
-    def join(self, other):
-        if self.sharing.able:
-            self.send = jnp.concatenate([self.send, other.send], axis=0)
+            self.send = jnp.concatenate([send, *got])
+
+    def split(self, parts):
+        self.keep, self.send = parts[0], parts[1:]
+
+    def half(self):
+        if not self.stages:
+            return
+        if self.ready is None:
+            self.ready = self.keep[4:8] + self.sharing.swap(self.send[4:8], *FIRST)
+            self.keep, self.send = self.keep[0:4], self.send[0:4]
         else:
-            self.keep = jnp.concatenate([self.keep, other.keep], axis=1)
-            self.send = jnp.concatenate([self.send, other.send], axis=1)
+            self.keep = self.keep + self.sharing.swap(self.send, *FIRST)
+            self.send, self.ready = self.ready, None
+            self.stages.pop(0)
 
     def result(self):
         return [self.keep, self.send]
+
+
+def advance(*chains):
+    chains = [chain for chain in chains if chain.stages]
+    offered = [chain.offers() for chain in chains]
+    got = [[None] * len(offers) for offers in offered]
+    partners = {}
+    for i, offers in enumerate(offered):
+        for j, (partner, _) in enumerate(offers):
+            partners.setdefault((partner, i if partner == CORE else 0), []).append((i, j))
+    for (partner, _), places in partners.items():
+        values = [offered[i][j][1] for i, j in places]
+        flat = [value.reshape(-1, 128) for value in values]
+        arrived = chains[0].sharing.swap(flat[0] if len(flat) == 1 else jnp.concatenate(flat), *partner)
+        at = 0
+        for (i, j), value, rows in zip(places, values, flat):
+            got[i][j] = arrived[at : at + rows.shape[0]].reshape(value.shape)
+            at += rows.shape[0]
+    for chain, received in zip(chains, got):
+        chain.accept(received)
 
 
 def shards(sizes, *arguments):
@@ -1062,7 +1131,6 @@
             where + [za, suma, pars[index][0], sumb, spatials[index][0], narrows[index][0]],
             [struct((r, 1536), LOW), struct((r, 384), LOW), struct((r, 512), F32), struct((2, 896), F32)],
             [around(layer, 3), pltpu.VMEM((r, 256), F32)],
-            flops=2 * r * 27 * 160 * 320,
             name="conv_forward",
         )
 
@@ -1073,6 +1141,7 @@
             where + [gu, zb, zc, suma, sums, back, pars[index][1]],
             [struct((r, 384), LOW), struct((r, 1024), LOW), struct((r, 384), LOW)],
             [around(layer, 1), pltpu.VMEM((r, 128), F32)],
+            fetch=[2, 3, 4] if layer.halved else [],
             name="unit_backward",
         )
 
@@ -1089,14 +1158,14 @@
                 pltpu.VMEM((r, 256), F32),
                 pltpu.VMEM((r, 128), F32),
             ],
-            flops=2 * r * 27 * 160 * 320,
+            late=[7, 8] if layer.halved else [],
             name="conv_backward",
         )
 
     sharing = Sharing(sizes)
     me = sharing.me()
 
-    def make_weights(index, columns, kinds, *operands, short=False):
+    def make_weights(index, columns, kinds, *operands, short=False, fetch=False):
         part = PARTS[index]
         scratch = []
         for kind in kinds:
@@ -1112,20 +1181,35 @@
             [struct((16, part[0], 128), F32)] * 2,
             [pltpu.VMEM(shape, F32) for shape in scratch],
             scalars=1,
-            flops=2 * operands[0].shape[0] * 32 * part[0] * 128,
+            fetch=range(1, 1 + len(operands)) if fetch else [],
             name="weights",
         )
         return Chain(sharing, *made, short=short)
 
+    def unit_and_first(layer, gu, zb, zc, suma, sums, back, index, wide, dza, upper_source, thin, source):
+        r = layer.rows
+        parts, columns = PARTS[1:3], ([(0, 2), (2, 2), (6, 1)], [(4, 2), (7, 1)])
+        pieces = [struct((16, part[0], 128), F32) for part in parts for _ in (0, 1)]
+        grads = [(1440, 640), (192, 896), (1440, 384), (384, 384), (832, 384)]
+        *made, keep, send, other_keep, other_send = call(
+            functools.partial(unit_and_weights, layer, parts, columns),
+            where + [me, gu, zb, zc, suma, sums, back, pars[index][1], wide, dza, upper_source, thin, source],
+            [struct((r, 384), LOW), struct((r, 1024), LOW), struct((r, 384), LOW)] + pieces,
+            [around(layer, 1), pltpu.VMEM((r, 128), F32)] + [pltpu.VMEM(shape, F32) for shape in grads],
+            scalars=3,
+            name="unit_and_weights",
+        )
+        return made, Chain(sharing, keep, send), Chain(sharing, other_keep, other_send)
+
     r0, r1 = lower.rows, upper.rows
     za, suma = call(
         functools.partial(first_a, lower), where + [x, points[0][0]],
-        [struct((r0, 384), F32), struct((3, 384), F32)], flops=2 * r0 * 832 * 384, name="first_a",
+        [struct((r0, 384), F32), struct((3, 384), F32)], name="first_a",
     )
     suma = sum_all(suma, sizes)
     zb, sumb = call(
         functools.partial(first_b, lower), where + [x, points[0][1]],
-        [struct((r0, 384), F32), struct((2, 384), F32)], [around(lower, 1)], flops=2 * r0 * 832 * 384, name="first_b",
+        [struct((r0, 384), F32), struct((2, 384), F32)], [around(lower, 1)], name="first_b",
     )
     wide, thin, zc, sums = forward(lower, za, suma, sumb, 0)
     sums = sum_all(sums, sizes)
@@ -1134,7 +1218,6 @@
         where + [zb, zc, suma, sums, pars[0][1], *points[1]],
         [struct((r1, 896), LOW), struct((r1, 384), F32), struct((r1, 384), F32), struct((3, 384), F32), struct((2, 384), F32)],
         [around(upper, 1), pltpu.VMEM((lower.frame, 1792), LOW)],
-        flops=2 * r1 * 832 * 768,
         name="finish_lower",
     )
     suma2 = sum_all(suma2, sizes)
@@ -1154,83 +1237,76 @@
     one = make_weights(0, [(0, 2), (2, 2), (4, 2), (6, 2)], "wo", wide2, three2, thin2, thin32, q, dzb2)
     meet(small, one)
     small.step()
-    one.step()
+    advance(one)
     meet(small, one)
     backa2 = small.result()
-    one.step()
+    advance(one)
     dza2, gu, back = call(
         functools.partial(join_blocks, upper, lower),
         where + [gua2, za2, suma2, backa2, pars[1][0], dzb2, *points[1], zb, zc, suma, sums, pars[0][1]],
         [struct((r1, 384), LOW), struct((r0, 896), F32), struct((2, 896), F32)],
         [pltpu.VMEM((lower.frame, 896), F32)],
-        flops=2 * r1 * 832 * 768,
         name="join_blocks",
     )
     held = Held(sum_all(back, sizes))
     meet(held, one)
     back = held.array
-    one.step()
-    dzb, three, thin3 = unit_back(lower, gu, zb, zc, suma, sums, back, 0)
-    two = make_weights(1, [(0, 2), (2, 2), (6, 1)], "wl", wide, three, dza2, q)
+    advance(one)
+    (dzb, three, thin3), two, more = unit_and_first(
+        lower, gu, zb, zc, suma, sums, back, 0, wide, dza2, q, thin, x
+    )
     held = Held(three)
-    meet(one, two, held)
-    one.step()
-    two.step()
-    two.step()
+    meet(one, two, more, held)
+    advance(one)
+    advance(two)
+    advance(more)
+    advance(two)
     gua, backa = conv_back(lower, held.array, thin3, za, suma, 0)
-    held = Held(three), Held(backa)
-    meet(two, *held)
-    more = make_weights(2, [(4, 2), (7, 1)], "wo", wide, held[0].array, thin, thin3, x, dzb)
-    meet(one, more)
-    one.step()
-    two.step()
-    more.step()
-    more.step()
-    backa = sum_all(held[1].array, sizes)
+    small = Sum(backa, sizes)
+    meet(two, more, small)
+    more.half()
+    small.step()
+    small.step()
+    meet(one, more, small)
+    advance(one)
+    more.half()
+    advance(two)
+    backa = small.result()
     dza, da = call(
         functools.partial(last_back, lower),
         where + [gua, za, suma, backa, pars[0][0], dzb, *points[0]],
         [struct((r0, 384), LOW), struct((r0, 832), LOW)],
-        flops=2 * r0 * 832 * 768,
         name="last_back",
     )
-    final = make_weights(3, [], "l", dza, x, short=True)
+    held = Held(dza)
+    meet(one, two, more, held)
+    final = make_weights(3, [], "l", held.array, x, short=True)
+    advance(one, two, more)
+    advance(final)
     meet(one, two, more, final)
-    one.step()
-    two.step()
-    more.step()
-    final.step()
-    final.step()
+    advance(one, two, more, final)
+    meet(one, two, more, final)
+    advance(one, more, final)
+    advance(two)
+    advance(two)
+    meet(one, two, more, final)
+    joined = Held(assemble_call(me, [(PARTS[0], one.result())], [(which, 1, 0, 0) for which in (SINGLE, SPATIAL, NARROW, PROJECT)], None))
+    advance(two, more, final)
+    meet(two, more, final, joined)
+    joined.array = assemble_call(
+        me, [(PARTS[1], two.result())], [(SPATIAL, 0, 0, 18), (REDUCE, 1, 0, 0), (SQUEEZE, 1, 0, 0)], list(joined.array)
+    )
     da = Held(frames_back(da.reshape(lower.frames, lower.frame, width), lower))
     out = jnp.concatenate([out[:, 0:576], out[:, 640:896]], axis=1)
     out = out.reshape(upper.frames, upper.frame, width)[:, 0 : upper.side * upper.side]
     out = Held(frames_back(out, upper))
-    meet(one, two, more, final, da, out)
-    one.step()
-    two.step()
-    more.step()
-    final.step()
-    meet(one, two, more, final)
-    more.join(final)
-    one.step()
-    two.step()
-    two.step()
-    more.step()
-    meet(one, two, more)
-    joined = Held(assemble_call(me, [(PARTS[0], one.result())], [(which, 1, 0, 0) for which in (SINGLE, SPATIAL, NARROW, PROJECT)], None))
-    two.step()
-    more.step()
-    more.step()
-    meet(two, more, joined)
-    joined.array = assemble_call(
-        me, [(PARTS[1], two.result())], [(SPATIAL, 0, 0, 18), (REDUCE, 1, 0, 0), (SQUEEZE, 1, 0, 0)], list(joined.array)
-    )
-    more.step()
-    meet(more, joined)
+    advance(more, final)
+    meet(more, final, joined, da, out)
+    advance(more, final)
     joined = list(joined.array)
     joined = list(assemble_call(
         me,
-        [(joined_part(PARTS[2], PARTS[3]), more.result())],
+        [(PARTS[2], more.result()), (PARTS[3], final.result())],
         [(SPATIAL, 0, 18, 9)] + [(which, 0, 0, 0) for which in (SINGLE, REDUCE, SQUEEZE, NARROW, PROJECT)],
         joined,
     ))

time: 379 us -> 351 us (0.926)
  waiting for transfers between devices: 143 us -> 129 us
  starting transfers between devices: 113 us -> 105 us
  local copies, waits for them, and re-layouts: 29.5 us -> 21.6 us
    ppermute x43 -> x42, waiting for transfers between devices: 95.1 us -> 79.9 us  [swap(): lax.ppermute(value, AXES, [(i, i ^ masks[i & 1]) for i in range(self.tota...]
    unnamed x116 -> x125, local copies, waits for them, and re-layouts: 22.9 us -> 13.9 us
    ppermute x43 -> x42, starting transfers between devices: 45 us -> 39.7 us  [swap(): lax.ppermute(value, AXES, [(i, i ^ masks[i & 1]) for i in range(self.tota...]
    pallas_call x16 -> x14, Pallas kernels: 68.1 us -> 68.6 us  [call(): pl.pallas_call(body, out_shape=tuple(outs), in_specs=specs, out_specs=tup...]
  transfers between devices with their start and end apart: 99 -> 98, of which waited for: 61 -> 61; matrix products, arithmetic and copies ran while one was open for 2% -> 2% of each run, Pallas kernels for 13% -> 15%
where the time goes in v1:
time: 351 us; the launch traced here: 347 us
  waiting for transfers between devices  129 us (37%)
  starting transfers between devices  105 us (30%)
  Pallas kernels  84.7 us (24%)
  local copies, waits for them, and re-layouts  21.6 us (6%)
  other arithmetic  4.4 us (1%)
    ppermute x42, waiting for transfers between devices, swap(): lax.ppermute(value, AXES, [(i, i ^ masks[i & 1]) for i in range(self.tota...  79.9 us
    pallas_call x14, Pallas kernels, call(): pl.pallas_call(body, out_shape=tuple(outs), in_specs=specs, out_specs=tup...  68.6 us
    ppermute x56, starting transfers between devices, swap(): return lax.ppermute(value, AXES, [(i, i ^ mask) for i in range(total)])  64.9 us
    ppermute x56, waiting for transfers between devices, swap(): return lax.ppermute(value, AXES, [(i, i ^ mask) for i in range(total)])  48.8 us
    ppermute x42, starting transfers between devices, swap(): lax.ppermute(value, AXES, [(i, i ^ masks[i & 1]) for i in range(self.tota...  39.7 us
    unnamed x125, local copies, waits for them, and re-layouts  13.9 us
    pallas_call x3, Pallas kernels, assemble_call(): pl.pallas_call(functools.partial(assemble, [(part, len(found) == 2) for p...  10.4 us
  transfers between devices with their start and end apart: 98, of which 61 were waited for; matrix products, arithmetic and copies ran while one was open for 2% of the time, Pallas kernels for 15%

profile of v1, /device:TPU:0, one launch (start us, length us, event | category | flops | bytes accessed | tf_op | source)
XLA Modules:
  0.0 347.1 jit_solution(2658144148342267545)
XLA Ops:
  1.3 2.3 copy.34
  4.5 2.4 first_a.1
  9.2 3.8 %collective-permute-start.3 = (f32[3,384]{1,0:T(4,128)S(1)}, f32[3,384]{1,0:T(4,128)S(1)}, u32[]{:S(2)}, u32[]{:S(2)}) collective-permute-start(f32[3,384]{1,0:T(4,128)S(1)} %add.335), channel_id=1, source_target_pairs={{0,6},{1,7},{2,4},{3,5},{4,2},{5,3},{6,0},{7,1},{8,14},{9,15},{10,... | collective-permute-start | bytes 13832 | tf_op jit(solution)/shard_map/ppermute | solution.py:917
  17.1 3.6 %collective-permute-start.6 = (f32[3,384]{1,0:T(4,128)S(1)}, f32[3,384]{1,0:T(4,128)S(1)}, u32[]{:S(2)}, u32[]{:S(2)}) collective-permute-start(f32[3,384]{1,0:T(4,128)S(1)} %add_add_fusion.13), channel_id=1, source_target_pairs={{0,24},{1,25},{2,26},{3,27},{4,28},{5,29},{6,30},{7,31},{8,16},{9,... | collective-permute-start | bytes 13832 | tf_op jit(solution)/shard_map/ppermute | solution.py:917
  21.5 2.9 first_b.1
  28.9 10.4 %conv_forward.2 = (bf16[1600,1536]{1,0:T(8,128)(2,1)S(1)}, bf16[1600,384]{1,0:T(8,128)(2,1)S(1)}, f32[1600,512]{1,0:T(8,128)S(1)}, f32[2,896]{1,0:T(2,128)S(1)}) custom-call(s32[1]{0:T(128)S(6)} %copy.56.group_ref.refs_0_, s32[3]{0:T(128)S(1)} %copy-done.45, f32[1600,384]{1,0:T(8,128)S(1)} %get-tuple-element.166.za_ref, ...), custom_call_target="tpu_custom_call" | custom-call | flops 1 | bytes 1 | tf_op jit(solution)/shard_map/conv_forward/pallas_call | solution.py:71
  39.3 2.2 copy-done.6
  48.2 3.8 %collective-permute-start.13 = (f32[2,896]{1,0:T(2,128)S(1)}, f32[2,896]{1,0:T(2,128)S(1)}, u32[]{:S(2)}, u32[]{:S(2)}) collective-permute-start(f32[2,896]{1,0:T(2,128)S(1)} %add_add_fusion.9), channel_id=1, source_target_pairs={{0,24},{1,25},{2,26},{3,27},{4,28},{5,29},{6,30},{7,31},{8,16},{9,... | collective-permute-start | bytes 21512 | tf_op jit(solution)/shard_map/ppermute | solution.py:917
  54.1 2.5 collective-permute-done.12
  56.7 4.6 %finish_lower.1 = (bf16[224,896]{1,0:T(8,128)(2,1)S(1)}, f32[224,384]{1,0:T(8,128)S(1)}, f32[224,384]{1,0:T(8,128)S(1)}, f32[3,384]{1,0:T(4,128)S(1)}, f32[2,384]{1,0:T(2,128)S(1)}) custom-call(s32[1]{0:T(128)S(6)} %copy.56.group_ref.refs_0_, s32[3]{0:T(128)S(1)} %copy-done.45, f32[1600,384]{1,0:T(8,128)S(1)} %get-tuple-element.164.zb_ref, ...), custom_call_target="tpu_custom_call" | custom-call | flops 1 | bytes 1 | tf_op jit(solution)/shard_map/finish_lower/pallas_call | solution.py:71
  62.5 2.5 collective-permute-start.17
  71.2 2.3 collective-permute-start.18
  75.2 2.2 conv_forward.3
  85.7 2.6 collective-permute-start.27
  96.1 2.5 collective-permute-start.31
  110.4 4.5 %conv_backward.2 = (f32[224,384]{1,0:T(8,128)S(1)}, f32[2,384]{1,0:T(2,128)}) custom-call(s32[1]{0:T(128)S(6)} %copy.56.group_ref.refs_0_, s32[3]{0:T(128)S(1)} %copy-done.45, bf16[224,1024]{1,0:T(8,128)(2,1)S(1)} %get-tuple-element.189.refs_2_.refs_1_, bf16[224,384]{1,0:T(8,128)(2,1)S(1)} %get-tuple-element.190.refs_3_, ...), custom_call_target="tpu_custom_call" | custom-call | flops 1 | bytes 1 | tf_op jit(solution)/shard_map/conv_backward/pallas_call | solution.py:71
  130.7 2.5 collective-permute-start.42
  137.9 5.1 %join_blocks.1 = (bf16[224,384]{1,0:T(8,128)(2,1)S(1)}, f32[1600,896]{1,0:T(8,128)S(1)}, f32[2,896]{1,0:T(2,128)S(1)}) custom-call(s32[1]{0:T(128)S(6)} %copy.56.group_ref.refs_0_, s32[3]{0:T(128)S(1)} %copy-done.46, f32[224,384]{1,0:T(8,128)S(1)} %copy-done.34, f32[224,384]{1,0:T(8,128)S(1)} %get-tuple-element.178.za_ref.refs_4_, f32[3,384]{1,0:T(4,128)S(1)} %copy-done.40, ...), custom_call_target="tpu_custom_call" | custom-call | flops 1 | bytes 1 | tf_op jit(solution)/shard_map/join_blocks/pallas_call | solution.py:71
  144.3 2.2 collective-permute-start.46
  147.8 7.6 %collective-permute-done.46 = f32[2,896]{1,0:T(2,128)S(1)} collective-permute-done((f32[2,896]{1,0:T(2,128)S(1)}, f32[2,896]{1,0:T(2,128)S(1)}, u32[]{:S(2)}, u32[]{:S(2)}) %collective-permute-start.46) | collective-permute-done | bytes 7200 | tf_op jit(solution)/shard_map/ppermute | solution.py:917
  155.4 2.6 collective-permute-start.49
  164.3 12.3 %unit_and_weights.1 = (bf16[1600,384]{1,0:T(8,128)(2,1)S(1)}, bf16[1600,1024]{1,0:T(8,128)(2,1)S(1)}, bf16[1600,384]{1,0:T(8,128)(2,1)S(1)}, f32[16,272,128]{2,1...) custom-call(s32[1]{0:T(128)S(6)} %copy.56.group_ref.refs_0_, ...), custom_call_target="tpu_custom_call" | custom-call | flops 1 | bytes 1 | tf_op jit(solution)/shard_map/unit_and_weights/pallas_call | solution.py:71
  177.7 3.8 %collective-permute-done.55 = f32[4352,128]{1,0:T(8,128)S(1)} collective-permute-done((f32[4352,128]{1,0:T(8,128)S(1)}, f32[4352,128]{1,0:T(8,128)S(1)}, u32[]{:S(2)}, u32[]{:S(2)}) %collective-permute-start.55) | collective-permute-done | bytes 2228256 | tf_op jit(solution)/shard_map/ppermute | solution.py:984
  184.8 2.4 collective-permute-start.54
  187.2 13.4 %conv_backward.3 = (f32[1600,384]{1,0:T(8,128)S(1)}, f32[2,384]{1,0:T(2,128)S(1)}) custom-call(s32[1]{0:T(128)S(6)} %copy.56.group_ref.refs_0_, s32[3]{0:T(128)S(1)} %copy-done.46, bf16[1600,1024]{1,0:T(8,128)(2,1)S(1)} %get-tuple-element.228.three_ref, bf16[1600,384]{1,0:T(8,128)(2,1)S(1)} %get-tuple-element.229.thin3_ref, f32[1600,384]{1,0:T(8,128)S(1)} %copy-done.5, ...), custom_call_target="tpu_custom_call" | custom-call | flops 1 | bytes 1 | tf_op jit(solution)/shard_map/conv_backward/pallas_call | solution.py:71
  208.1 3.3 collective-permute-done.62
  213.0 3.0 collective-permute-start.68
  217.4 2.2 collective-permute-done.69
  222.0 4.5 %last_back.1 = (bf16[1600,384]{1,0:T(8,128)(2,1)S(1)}, bf16[1600,832]{1,0:T(8,128)(2,1)S(1)}) custom-call(s32[1]{0:T(128)S(6)} %copy.56.group_ref.refs_0_, s32[3]{0:T(128)S(1)} %copy-done.46, f32[1600,384]{1,0:T(8,128)S(1)} %get-tuple-element.242.gua_ref, f32[1600,384]{1,0:T(8,128)S(1)} %copy-done.5, f32[3,384]{1,0:T(4,128)S(1)} %copy-done.36, ...), custom_call_target="tpu_custom_call" | custom-call | flops 1 | bytes 1 | tf_op jit(solution)/shard_map/last_back/pallas_call | solution.py:71
  227.8 7.6 %collective-permute-done.63 = f32[472,128]{1,0:T(8,128)S(1)} collective-permute-done((f32[472,128]{1,0:T(8,128)S(1)}, f32[472,128]{1,0:T(8,128)S(1)}, u32[]{:S(2)}, u32[]{:S(2)}) %collective-permute-start.63) | collective-permute-done | bytes 241696 | tf_op jit(solution)/shard_map/ppermute | solution.py:984
  238.8 2.3 collective-permute-start.73
  241.1 2.1 collective-permute-start.74
  243.1 5.0 %collective-permute-done.72 = f32[272,128]{1,0:T(8,128)S(1)} collective-permute-done((f32[272,128]{1,0:T(8,128)S(1)}, f32[272,128]{1,0:T(8,128)S(1)}, u32[]{:S(2)}, u32[]{:S(2)}) %collective-permute-start.72) | collective-permute-done | bytes 139296 | tf_op jit(solution)/shard_map/ppermute | solution.py:984
  248.1 2.9 collective-permute-done.73
  251.2 3.8 %collective-permute-done.71 = f32[2848,128]{1,0:T(8,128)S(1)} collective-permute-done((f32[2848,128]{1,0:T(8,128)S(1)}, f32[2848,128]{1,0:T(8,128)S(1)}, u32[]{:S(2)}, u32[]{:S(2)}) %collective-permute-start.71) | collective-permute-done | bytes 1458208 | tf_op jit(solution)/shard_map/ppermute | solution.py:984
  261.2 8.1 %collective-permute-done.77 = f32[512,128]{1,0:T(8,128)S(1)} collective-permute-done((f32[512,128]{1,0:T(8,128)S(1)}, f32[512,128]{1,0:T(8,128)S(1)}, u32[]{:S(2)}, u32[]{:S(2)}) %collective-permute-start.77) | collective-permute-done | bytes 262176 | tf_op jit(solution)/shard_map/ppermute | solution.py:984
  270.0 7.5 %collective-permute-done.79 = f32[512,128]{1,0:T(8,128)S(1)} collective-permute-done((f32[512,128]{1,0:T(8,128)S(1)}, f32[512,128]{1,0:T(8,128)S(1)}, u32[]{:S(2)}, u32[]{:S(2)}) %collective-permute-start.79) | collective-permute-done | bytes 262176 | tf_op jit(solution)/shard_map/ppermute | solution.py:984
  277.6 5.0 %collective-permute-done.76 = f32[3968,128]{1,0:T(8,128)S(1)} collective-permute-done((f32[3968,128]{1,0:T(8,128)S(1)}, f32[3968,128]{1,0:T(8,128)S(1)}, u32[]{:S(2)}, u32[]{:S(2)}) %collective-permute-start.76) | collective-permute-done | bytes 2031648 | tf_op jit(solution)/shard_map/ppermute | solution.py:984
  285.8 8.2 %collective-permute-done.83 = f32[1088,128]{1,0:T(8,128)S(1)} collective-permute-done((f32[1088,128]{1,0:T(8,128)S(1)}, f32[1088,128]{1,0:T(8,128)S(1)}, u32[]{:S(2)}, u32[]{:S(2)}) %collective-permute-start.83) | collective-permute-done | bytes 557088 | tf_op jit(solution)/shard_map/ppermute | solution.py:984
  297.0 4.6 %collective-permute-done.86 = f32[288,128]{1,0:T(8,128)S(1)} collective-permute-done((f32[288,128]{1,0:T(8,128)S(1)}, f32[288,128]{1,0:T(8,128)S(1)}, u32[]{:S(2)}, u32[]{:S(2)}) %collective-permute-start.86) | collective-permute-done | bytes 147488 | tf_op jit(solution)/shard_map/ppermute | solution.py:984
  303.4 6.2 %collective-permute-done.84 = f32[2176,128]{1,0:T(8,128)S(1)} collective-permute-done((f32[2176,128]{1,0:T(8,128)S(1)}, f32[2176,128]{1,0:T(8,128)S(1)}, u32[]{:S(2)}, u32[]{:S(2)}) %collective-permute-start.84) | collective-permute-done | bytes 1114144 | tf_op jit(solution)/shard_map/ppermute | solution.py:984
  312.3 2.9 collective-permute-start.90
  315.2 3.8 %assemble.3 = (f32[2,832,256]{2,1,0:T(8,128)}, f32[2,160,832]{2,1,0:T(8,128)}, f32[2,27,160,320]{3,2,1,0:T(8,128)}, f32[2,32,832]{2,1,0:T(8,128)}, f32[2,27,32,128]{3,2,1,0:T(8,128)}, /*index=5*/f32[2,832,128]{2,1,0:T(8,128)}) custom-call(s32[1]{0:T(128)} %bitcast.13.me_ref, f32[16,472,128]{2,1,0:T(8,128)S(1)} %pad_maximum_fusion.refs_0_, ...), custom_call_target="tpu_custom_call" | custom-call | flops 1 | bytes 1 | tf_op jit(solution)/shard_map/assemble/pallas_call | solution.py:781
  321.8 2.7 copy.36
  326.7 2.7 assemble.4
  329.4 7.2 %collective-permute-done.93 = f32[2112,128]{1,0:T(8,128)S(1)} collective-permute-done((f32[2112,128]{1,0:T(8,128)S(1)}, f32[2112,128]{1,0:T(8,128)S(1)}, u32[]{:S(2)}, u32[]{:S(2)}) %collective-permute-start.93) | collective-permute-done | bytes 1081376 | tf_op jit(solution)/shard_map/ppermute | solution.py:984
  339.8 2.9 collective-permute-done.97
  343.0 3.9 %assemble.5 = (f32[2,832,256]{2,1,0:T(8,128)}, f32[2,160,832]{2,1,0:T(8,128)}, f32[2,27,160,320]{3,2,1,0:T(8,128)}, f32[2,32,832]{2,1,0:T(8,128)}, f32[2,27,32,128]{3,2,1,0:T(8,128)}, /*index=5*/f32[2,832,128]{2,1,0:T(8,128)}) custom-call(s32[1]{0:T(128)} %bitcast.13.me_ref, ...), custom_call_target="tpu_custom_call", output_to_operand_aliasing={{0}: (5, {}), {1}: (6, {}), {2}: (7, {}), {3}: (8, {}), {4}... | custom-call | flops 1 | bytes 1 | tf_op jit(solution)/shard_map/assemble/pallas_call | solution.py:781
  (400 shorter events, 134.8 us)
Async XLA Ops:
  17.1 11.7 %collective-permute-start.6 = (f32[3,384]{1,0:T(4,128)S(1)}, f32[3,384]{1,0:T(4,128)S(1)}, u32[]{:S(2)}, u32[]{:S(2)}) collective-permute-start(f32[3,384]{1,0:T(4,128)S(1)} %add_add_fusion.13), channel_id=1, source_target_pairs={{0,24},{1,25},{2,26},{3,27},{4,28},{5,29},{6,30},{7,31},{8,16},{9,... | collective-permute-start | bytes 13832 | tf_op jit(solution)/shard_map/ppermute | solution.py:917
  20.7 8.1 %collective-permute-start.5 = (f32[3,384]{1,0:T(4,128)S(1)}, f32[3,384]{1,0:T(4,128)S(1)}, u32[]{:S(2)}, u32[]{:S(2)}) collective-permute-start(f32[3,384]{1,0:T(4,128)S(1)} %add_add_fusion.13), channel_id=1, source_target_pairs={{0,16},{1,17},{2,18},{3,19},{4,20},{5,21},{6,22},{7,23},{8,24},{9,... | collective-permute-start | bytes 13832 | tf_op jit(solution)/shard_map/ppermute | solution.py:917
  20.7 8.1 %collective-permute-start.4 = (f32[3,384]{1,0:T(4,128)S(1)}, f32[3,384]{1,0:T(4,128)S(1)}, u32[]{:S(2)}, u32[]{:S(2)}) collective-permute-start(f32[3,384]{1,0:T(4,128)S(1)} %add_add_fusion.13), channel_id=1, source_target_pairs={{0,8},{1,9},{2,10},{3,11},{4,12},{5,13},{6,14},{7,15},{8,0},{9,1},... | collective-permute-start | bytes 13832 | tf_op jit(solution)/shard_map/ppermute | solution.py:917
  122.3 6.8 %collective-permute-start.39 = (f32[7552,128]{1,0:T(8,128)S(1)}, f32[7552,128]{1,0:T(8,128)S(1)}, u32[]{:S(2)}, u32[]{:S(2)}) collective-permute-start(f32[7552,128]{1,0:T(8,128)S(1)} %bitcast.167), channel_id=1, source_target_pairs={{0,1},{1,0},{2,3},{3,2},{4,5},{5,4},{6,7},{7,6},{8,9},{9,8},{10,11... | collective-permute-start | bytes 11599880 | tf_op jit(solution)/shard_map/ppermute | solution.py:984
  129.9 32.8 %collective-permute-start.50 = (f32[3776,128]{1,0:T(8,128)S(1)}, f32[3776,128]{1,0:T(8,128)S(1)}, u32[]{:S(2)}, u32[]{:S(2)}) collective-permute-start(f32[3776,128]{1,0:T(8,128)S(1)} %bitcast.197), channel_id=1, source_target_pairs={{0,2},{1,5},{2,0},{3,7},{4,6},{5,1},{6,4},{7,3},{8,10},{9,13},{10,... | collective-permute-start | bytes 5799944 | tf_op jit(solution)/shard_map/ppermute | solution.py:984
  144.3 11.1 %collective-permute-start.46 = (f32[2,896]{1,0:T(2,128)S(1)}, f32[2,896]{1,0:T(2,128)S(1)}, u32[]{:S(2)}, u32[]{:S(2)}) collective-permute-start(f32[2,896]{1,0:T(2,128)S(1)} %add.384), channel_id=1, source_target_pairs={{0,6},{1,7},{2,4},{3,5},{4,2},{5,3},{6,0},{7,1},{8,14},{9,15},{10,... | collective-permute-start | bytes 21512 | tf_op jit(solution)/shard_map/ppermute | solution.py:917
  146.5 8.9 %collective-permute-start.45 = (f32[2,896]{1,0:T(2,128)S(1)}, f32[2,896]{1,0:T(2,128)S(1)}, u32[]{:S(2)}, u32[]{:S(2)}) collective-permute-start(f32[2,896]{1,0:T(2,128)S(1)} %add.384), channel_id=1, source_target_pairs={{0,4},{1,5},{2,6},{3,7},{4,0},{5,1},{6,2},{7,3},{8,12},{9,13},{10,... | collective-permute-start | bytes 21512 | tf_op jit(solution)/shard_map/ppermute | solution.py:917
  147.0 8.4 %collective-permute-start.44 = (f32[2,896]{1,0:T(2,128)S(1)}, f32[2,896]{1,0:T(2,128)S(1)}, u32[]{:S(2)}, u32[]{:S(2)}) collective-permute-start(f32[2,896]{1,0:T(2,128)S(1)} %add.384), channel_id=1, source_target_pairs={{0,2},{1,3},{2,0},{3,1},{4,6},{5,7},{6,4},{7,5},{8,10},{9,11},{10,... | collective-permute-start | bytes 21512 | tf_op jit(solution)/shard_map/ppermute | solution.py:917
  163.0 14.0 %collective-permute-start.51 = (f32[1888,128]{1,0:T(8,128)S(1)}, f32[1888,128]{1,0:T(8,128)S(1)}, u32[]{:S(2)}, u32[]{:S(2)}) collective-permute-start(f32[1888,128]{1,0:T(8,128)S(1)} %bitcast.206), channel_id=1, source_target_pairs={{0,4},{1,3},{2,6},{3,1},{4,0},{5,7},{6,2},{7,5},{8,12},{9,11},{10,... | collective-permute-start | bytes 2899976 | tf_op jit(solution)/shard_map/ppermute | solution.py:984
  177.2 23.5 %collective-permute-start.57 = (f32[3840,128]{1,0:T(8,128)S(1)}, f32[3840,128]{1,0:T(8,128)S(1)}, u32[]{:S(2)}, u32[]{:S(2)}) collective-permute-start(f32[3840,128]{1,0:T(8,128)S(1)} %bitcast.169), channel_id=1, source_target_pairs={{0,1},{1,0},{2,3},{3,2},{4,5},{5,4},{6,7},{7,6},{8,9},{9,8},{10,11... | collective-permute-start | bytes 5898248 | tf_op jit(solution)/shard_map/ppermute | solution.py:984
  182.0 19.1 %collective-permute-start.56 = (f32[2176,128]{1,0:T(8,128)S(1)}, f32[2176,128]{1,0:T(8,128)S(1)}, u32[]{:S(2)}, u32[]{:S(2)}) collective-permute-start(f32[2176,128]{1,0:T(8,128)S(1)} %bitcast.202), channel_id=1, source_target_pairs={{0,2},{1,5},{2,0},{3,7},{4,6},{5,1},{6,4},{7,3},{8,10},{9,13},{10,... | collective-permute-start | bytes 3342344 | tf_op jit(solution)/shard_map/ppermute | solution.py:984
  182.8 21.9 %collective-permute-start.52 = (f32[472,128]{1,0:T(8,128)S(1)}, f32[472,128]{1,0:T(8,128)S(1)}, u32[]{:S(2)}, u32[]{:S(2)}) collective-permute-start(f32[472,128]{1,0:T(8,128)S(1)} %get-tuple-element.221), channel_id=1, source_target_pairs={{0,16},{1,17},{2,18},{3,19},{4,20},{5,21},{6,22},{7,23},{8,24},{9,... | collective-permute-start | bytes 725000 | tf_op jit(solution)/shard_map/ppermute | solution.py:984
  184.8 21.3 %collective-permute-start.53 = (f32[472,128]{1,0:T(8,128)S(1)}, f32[472,128]{1,0:T(8,128)S(1)}, u32[]{:S(2)}, u32[]{:S(2)}) collective-permute-start(f32[472,128]{1,0:T(8,128)S(1)} %get-tuple-element.222), channel_id=1, source_target_pairs={{0,8},{1,9},{2,10},{3,11},{4,12},{5,13},{6,14},{7,15},{8,0},{9,1},... | collective-permute-start | bytes 725000 | tf_op jit(solution)/shard_map/ppermute | solution.py:984
  184.8 22.6 %collective-permute-start.54 = (f32[472,128]{1,0:T(8,128)S(1)}, f32[472,128]{1,0:T(8,128)S(1)}, u32[]{:S(2)}, u32[]{:S(2)}) collective-permute-start(f32[472,128]{1,0:T(8,128)S(1)} %get-tuple-element.223), channel_id=1, source_target_pairs={{0,24},{1,25},{2,26},{3,27},{4,28},{5,29},{6,30},{7,31},{8,16},{9,... | collective-permute-start | bytes 725000 | tf_op jit(solution)/shard_map/ppermute | solution.py:984
  201.4 10.0 %collective-permute-start.58 = (f32[4,240,128]{2,1,0:T(8,128)S(1)}, f32[4,240,128]{2,1,0:T(8,128)S(1)}, u32[]{:S(2)}, u32[]{:S(2)}) collective-permute-start(f32[4,240,128]{2,1,0:T(8,128)S(1)} %get-tuple-element.354), channel_id=1, source_target_pairs={{0,2},{1,5},{2,0},{3,7},{4,6},{5,1},{6,4},{7,3},{8,10},{9,13},{10,... | collective-permute-start | bytes 1474568 | tf_op jit(solution)/shard_map/ppermute | solution.py:984
  203.8 7.5 %collective-permute-start.62 = (f32[2,384]{1,0:T(2,128)S(1)}, f32[2,384]{1,0:T(2,128)S(1)}, u32[]{:S(2)}, u32[]{:S(2)}) collective-permute-start(f32[2,384]{1,0:T(2,128)S(1)} %add.407), channel_id=1, source_target_pairs={{0,6},{1,7},{2,4},{3,5},{4,2},{5,3},{6,0},{7,1},{8,14},{9,15},{10,... | collective-permute-start | bytes 9224 | tf_op jit(solution)/shard_map/ppermute | solution.py:917
  204.7 6.7 %collective-permute-start.61 = (f32[2,384]{1,0:T(2,128)S(1)}, f32[2,384]{1,0:T(2,128)S(1)}, u32[]{:S(2)}, u32[]{:S(2)}) collective-permute-start(f32[2,384]{1,0:T(2,128)S(1)} %add.407), channel_id=1, source_target_pairs={{0,4},{1,5},{2,6},{3,7},{4,0},{5,1},{6,2},{7,3},{8,12},{9,13},{10,... | collective-permute-start | bytes 9224 | tf_op jit(solution)/shard_map/ppermute | solution.py:917
  207.4 19.1 %collective-permute-start.66 = (f32[1088,128]{1,0:T(8,128)S(1)}, f32[1088,128]{1,0:T(8,128)S(1)}, u32[]{:S(2)}, u32[]{:S(2)}) collective-permute-start(f32[1088,128]{1,0:T(8,128)S(1)} %bitcast.214), channel_id=1, source_target_pairs={{0,4},{1,3},{2,6},{3,1},{4,0},{5,7},{6,2},{7,5},{8,12},{9,11},{10,... | collective-permute-start | bytes 1671176 | tf_op jit(solution)/shard_map/ppermute | solution.py:984
  213.0 6.6 %collective-permute-start.69 = (f32[2,384]{1,0:T(2,128)S(1)}, f32[2,384]{1,0:T(2,128)S(1)}, u32[]{:S(2)}, u32[]{:S(2)}) collective-permute-start(f32[2,384]{1,0:T(2,128)S(1)} %add_add_fusion.15), channel_id=1, source_target_pairs={{0,16},{1,17},{2,18},{3,19},{4,20},{5,21},{6,22},{7,23},{8,24},{9,... | collective-permute-start | bytes 9224 | tf_op jit(solution)/shard_map/ppermute | solution.py:917
  213.0 7.4 %collective-permute-start.68 = (f32[2,384]{1,0:T(2,128)S(1)}, f32[2,384]{1,0:T(2,128)S(1)}, u32[]{:S(2)}, u32[]{:S(2)}) collective-permute-start(f32[2,384]{1,0:T(2,128)S(1)} %add_add_fusion.15), channel_id=1, source_target_pairs={{0,8},{1,9},{2,10},{3,11},{4,12},{5,13},{6,14},{7,15},{8,0},{9,1},... | collective-permute-start | bytes 9224 | tf_op jit(solution)/shard_map/ppermute | solution.py:917
  215.9 10.7 %collective-permute-start.65 = (f32[472,128]{1,0:T(8,128)S(1)}, f32[472,128]{1,0:T(8,128)S(1)}, u32[]{:S(2)}, u32[]{:S(2)}) collective-permute-start(f32[472,128]{1,0:T(8,128)S(1)} %add_add_fusion), channel_id=1, source_target_pairs={{0,24},{1,25},{2,26},{3,27},{4,28},{5,29},{6,30},{7,31},{8,16},{9,... | collective-permute-start | bytes 725000 | tf_op jit(solution)/shard_map/ppermute | solution.py:984
  217.3 10.4 %collective-permute-start.64 = (f32[472,128]{1,0:T(8,128)S(1)}, f32[472,128]{1,0:T(8,128)S(1)}, u32[]{:S(2)}, u32[]{:S(2)}) collective-permute-start(f32[472,128]{1,0:T(8,128)S(1)} %add_add_fusion), channel_id=1, source_target_pairs={{0,8},{1,9},{2,10},{3,11},{4,12},{5,13},{6,14},{7,15},{8,0},{9,1},... | collective-permute-start | bytes 725000 | tf_op jit(solution)/shard_map/ppermute | solution.py:984
  219.6 15.9 %collective-permute-start.63 = (f32[472,128]{1,0:T(8,128)S(1)}, f32[472,128]{1,0:T(8,128)S(1)}, u32[]{:S(2)}, u32[]{:S(2)}) collective-permute-start(f32[472,128]{1,0:T(8,128)S(1)} %add_add_fusion), channel_id=1, source_target_pairs={{0,16},{1,17},{2,18},{3,19},{4,20},{5,21},{6,22},{7,23},{8,24},{9,... | collective-permute-start | bytes 725000 | tf_op jit(solution)/shard_map/ppermute | solution.py:984
  220.3 15.2 %collective-permute-start.67 = (f32[4,240,128]{2,1,0:T(8,128)S(1)}, f32[4,240,128]{2,1,0:T(8,128)S(1)}, u32[]{:S(2)}, u32[]{:S(2)}) collective-permute-start(f32[4,240,128]{2,1,0:T(8,128)S(1)} %get-tuple-element.240), channel_id=1, source_target_pairs={{0,2},{1,5},{2,0},{3,7},{4,6},{5,1},{6,4},{7,3},{8,10},{9,13},{10,... | collective-permute-start | bytes 1474568 | tf_op jit(solution)/shard_map/ppermute | solution.py:984
  235.7 19.3 %collective-permute-start.71 = (f32[2848,128]{1,0:T(8,128)S(1)}, f32[2848,128]{1,0:T(8,128)S(1)}, u32[]{:S(2)}, u32[]{:S(2)}) collective-permute-start(f32[2848,128]{1,0:T(8,128)S(1)} %pad_maximum_fusion.5), channel_id=1, source_target_pairs={{0,4},{1,3},{2,6},{3,1},{4,0},{5,7},{6,2},{7,5},{8,12},{9,11},{10,... | collective-permute-start | bytes 4374536 | tf_op jit(solution)/shard_map/ppermute | solution.py:984
  238.6 12.5 %collective-permute-start.75 = (f32[768,128]{1,0:T(8,128)S(1)}, f32[768,128]{1,0:T(8,128)S(1)}, u32[]{:S(2)}, u32[]{:S(2)}) collective-permute-start(f32[768,128]{1,0:T(8,128)S(1)} %bitcast.170), channel_id=1, source_target_pairs={{0,1},{1,0},{2,3},{3,2},{4,5},{5,4},{6,7},{7,6},{8,9},{9,8},{10,11... | collective-permute-start | bytes 1179656 | tf_op jit(solution)/shard_map/ppermute | solution.py:984
  238.7 9.4 %collective-permute-start.72 = (f32[272,128]{1,0:T(8,128)S(1)}, f32[272,128]{1,0:T(8,128)S(1)}, u32[]{:S(2)}, u32[]{:S(2)}) collective-permute-start(f32[272,128]{1,0:T(8,128)S(1)} %get-tuple-element.249), channel_id=1, source_target_pairs={{0,16},{1,17},{2,18},{3,19},{4,20},{5,21},{6,22},{7,23},{8,24},{9,... | collective-permute-start | bytes 417800 | tf_op jit(solution)/shard_map/ppermute | solution.py:984
  238.8 12.3 %collective-permute-start.73 = (f32[272,128]{1,0:T(8,128)S(1)}, f32[272,128]{1,0:T(8,128)S(1)}, u32[]{:S(2)}, u32[]{:S(2)}) collective-permute-start(f32[272,128]{1,0:T(8,128)S(1)} %get-tuple-element.250), channel_id=1, source_target_pairs={{0,8},{1,9},{2,10},{3,11},{4,12},{5,13},{6,14},{7,15},{8,0},{9,1},... | collective-permute-start | bytes 417800 | tf_op jit(solution)/shard_map/ppermute | solution.py:984
  241.1 10.0 %collective-permute-start.74 = (f32[272,128]{1,0:T(8,128)S(1)}, f32[272,128]{1,0:T(8,128)S(1)}, u32[]{:S(2)}, u32[]{:S(2)}) collective-permute-start(f32[272,128]{1,0:T(8,128)S(1)} %get-tuple-element.251), channel_id=1, source_target_pairs={{0,24},{1,25},{2,26},{3,27},{4,28},{5,29},{6,30},{7,31},{8,16},{9,... | collective-permute-start | bytes 417800 | tf_op jit(solution)/shard_map/ppermute | solution.py:984
  255.4 27.2 %collective-permute-start.76 = (f32[3968,128]{1,0:T(8,128)S(1)}, f32[3968,128]{1,0:T(8,128)S(1)}, u32[]{:S(2)}, u32[]{:S(2)}) collective-permute-start(f32[3968,128]{1,0:T(8,128)S(1)} %pad_maximum_fusion.2), channel_id=1, source_target_pairs={{0,2},{1,5},{2,0},{3,7},{4,6},{5,1},{6,4},{7,3},{8,10},{9,13},{10,... | collective-permute-start | bytes 6094856 | tf_op jit(solution)/shard_map/ppermute | solution.py:984
  256.8 12.5 %collective-permute-start.77 = (f32[512,128]{1,0:T(8,128)S(1)}, f32[512,128]{1,0:T(8,128)S(1)}, u32[]{:S(2)}, u32[]{:S(2)}) collective-permute-start(f32[512,128]{1,0:T(8,128)S(1)} %get-tuple-element.362), channel_id=1, source_target_pairs={{0,16},{1,17},{2,18},{3,19},{4,20},{5,21},{6,22},{7,23},{8,24},{9,... | collective-permute-start | bytes 786440 | tf_op jit(solution)/shard_map/ppermute | solution.py:984
  256.8 13.1 %collective-permute-start.78 = (f32[512,128]{1,0:T(8,128)S(1)}, f32[512,128]{1,0:T(8,128)S(1)}, u32[]{:S(2)}, u32[]{:S(2)}) collective-permute-start(f32[512,128]{1,0:T(8,128)S(1)} %get-tuple-element.363), channel_id=1, source_target_pairs={{0,8},{1,9},{2,10},{3,11},{4,12},{5,13},{6,14},{7,15},{8,0},{9,1},... | collective-permute-start | bytes 786440 | tf_op jit(solution)/shard_map/ppermute | solution.py:984
  258.9 24.1 %collective-permute-start.80 = (f32[192,128]{1,0:T(8,128)S(1)}, f32[192,128]{1,0:T(8,128)S(1)}, u32[]{:S(2)}, u32[]{:S(2)}) collective-permute-start(f32[192,128]{1,0:T(8,128)S(1)} %bitcast.225), channel_id=1, source_target_pairs={{0,4},{1,3},{2,6},{3,1},{4,0},{5,7},{6,2},{7,5},{8,12},{9,11},{10,... | collective-permute-start | bytes 294920 | tf_op jit(solution)/shard_map/ppermute | solution.py:984
  260.2 24.1 %collective-permute-start.81 = (f32[192,128]{1,0:T(8,128)S(1)}, f32[192,128]{1,0:T(8,128)S(1)}, u32[]{:S(2)}, u32[]{:S(2)}) collective-permute-start(f32[192,128]{1,0:T(8,128)S(1)} %bitcast.226), channel_id=1, source_target_pairs={{0,6},{1,7},{2,4},{3,5},{4,2},{5,3},{6,0},{7,1},{8,14},{9,15},{10,... | collective-permute-start | bytes 294920 | tf_op jit(solution)/shard_map/ppermute | solution.py:984
  269.3 8.2 %collective-permute-start.79 = (f32[512,128]{1,0:T(8,128)S(1)}, f32[512,128]{1,0:T(8,128)S(1)}, u32[]{:S(2)}, u32[]{:S(2)}) collective-permute-start(f32[512,128]{1,0:T(8,128)S(1)} %get-tuple-element.364), channel_id=1, source_target_pairs={{0,24},{1,25},{2,26},{3,27},{4,28},{5,29},{6,30},{7,31},{8,16},{9,... | collective-permute-start | bytes 786440 | tf_op jit(solution)/shard_map/ppermute | solution.py:984
  284.3 25.5 %collective-permute-start.82 = (f32[7552,128]{1,0:T(8,128)S(1)}, f32[7552,128]{1,0:T(8,128)S(1)}, u32[]{:S(2)}, u32[]{:S(2)}) collective-permute-start(f32[7552,128]{1,0:T(8,128)S(1)} %bitcast.150), channel_id=1, source_target_pairs={{0,1},{1,0},{2,3},{3,2},{4,5},{5,4},{6,7},{7,6},{8,9},{9,8},{10,11... | collective-permute-start | bytes 11599880 | tf_op jit(solution)/shard_map/ppermute | solution.py:984
  284.4 9.6 %collective-permute-start.83 = (f32[1088,128]{1,0:T(8,128)S(1)}, f32[1088,128]{1,0:T(8,128)S(1)}, u32[]{:S(2)}, u32[]{:S(2)}) collective-permute-start(f32[1088,128]{1,0:T(8,128)S(1)} %bitcast.178), channel_id=1, source_target_pairs={{0,4},{1,3},{2,6},{3,1},{4,0},{5,7},{6,2},{7,5},{8,12},{9,11},{10,... | collective-permute-start | bytes 1671176 | tf_op jit(solution)/shard_map/ppermute | solution.py:984
  285.3 11.6 %collective-permute-start.85 = (f32[288,128]{1,0:T(8,128)S(1)}, f32[288,128]{1,0:T(8,128)S(1)}, u32[]{:S(2)}, u32[]{:S(2)}) collective-permute-start(f32[288,128]{1,0:T(8,128)S(1)} %get-tuple-element.365), channel_id=1, source_target_pairs={{0,16},{1,17},{2,18},{3,19},{4,20},{5,21},{6,22},{7,23},{8,24},{9,... | collective-permute-start | bytes 442376 | tf_op jit(solution)/shard_map/ppermute | solution.py:984
  294.1 15.6 %collective-permute-start.84 = (f32[2176,128]{1,0:T(8,128)S(1)}, f32[2176,128]{1,0:T(8,128)S(1)}, u32[]{:S(2)}, u32[]{:S(2)}) collective-permute-start(f32[2176,128]{1,0:T(8,128)S(1)} %bitcast.204), channel_id=1, source_target_pairs={{0,2},{1,5},{2,0},{3,7},{4,6},{5,1},{6,4},{7,3},{8,10},{9,13},{10,... | collective-permute-start | bytes 3342344 | tf_op jit(solution)/shard_map/ppermute | solution.py:984
  295.0 8.4 %collective-permute-start.87 = (f32[288,128]{1,0:T(8,128)S(1)}, f32[288,128]{1,0:T(8,128)S(1)}, u32[]{:S(2)}, u32[]{:S(2)}) collective-permute-start(f32[288,128]{1,0:T(8,128)S(1)} %get-tuple-element.367), channel_id=1, source_target_pairs={{0,24},{1,25},{2,26},{3,27},{4,28},{5,29},{6,30},{7,31},{8,16},{9,... | collective-permute-start | bytes 442376 | tf_op jit(solution)/shard_map/ppermute | solution.py:984
  309.8 9.3 %collective-permute-start.88 = (f32[4352,128]{1,0:T(8,128)S(1)}, f32[4352,128]{1,0:T(8,128)S(1)}, u32[]{:S(2)}, u32[]{:S(2)}) collective-permute-start(f32[4352,128]{1,0:T(8,128)S(1)} %bitcast.151), channel_id=1, source_target_pairs={{0,1},{1,0},{2,3},{3,2},{4,5},{5,4},{6,7},{7,6},{8,9},{9,8},{10,11... | collective-permute-start | bytes 6684680 | tf_op jit(solution)/shard_map/ppermute | solution.py:984
  309.9 9.1 %collective-permute-start.89 = (f32[960,128]{1,0:T(8,128)S(1)}, f32[960,128]{1,0:T(8,128)S(1)}, u32[]{:S(2)}, u32[]{:S(2)}) collective-permute-start(f32[960,128]{1,0:T(8,128)S(1)} %bitcast.196), channel_id=1, source_target_pairs={{0,4},{1,3},{2,6},{3,1},{4,0},{5,7},{6,2},{7,5},{8,12},{9,11},{10,... | collective-permute-start | bytes 1474568 | tf_op jit(solution)/shard_map/ppermute | solution.py:984
  310.8 8.2 %collective-permute-start.92 = (f32[48,128]{1,0:T(8,128)S(1)}, f32[48,128]{1,0:T(8,128)S(1)}, u32[]{:S(2)}, u32[]{:S(2)}) collective-permute-start(f32[48,128]{1,0:T(8,128)S(1)} %fusion.1), channel_id=1, source_target_pairs={{0,24},{1,25},{2,26},{3,27},{4,28},{5,29},{6,30},{7,31},{8,16},{9,... | collective-permute-start | bytes 73736 | tf_op jit(solution)/shard_map/ppermute | solution.py:984
  312.3 6.7 %collective-permute-start.91 = (f32[48,128]{1,0:T(8,128)S(1)}, f32[48,128]{1,0:T(8,128)S(1)}, u32[]{:S(2)}, u32[]{:S(2)}) collective-permute-start(f32[48,128]{1,0:T(8,128)S(1)} %fusion.1), channel_id=1, source_target_pairs={{0,8},{1,9},{2,10},{3,11},{4,12},{5,13},{6,14},{7,15},{8,0},{9,1},... | collective-permute-start | bytes 73736 | tf_op jit(solution)/shard_map/ppermute | solution.py:984
  312.3 6.7 %collective-permute-start.90 = (f32[48,128]{1,0:T(8,128)S(1)}, f32[48,128]{1,0:T(8,128)S(1)}, u32[]{:S(2)}, u32[]{:S(2)}) collective-permute-start(f32[48,128]{1,0:T(8,128)S(1)} %fusion.1), channel_id=1, source_target_pairs={{0,16},{1,17},{2,18},{3,19},{4,20},{5,21},{6,22},{7,23},{8,24},{9,... | collective-permute-start | bytes 73736 | tf_op jit(solution)/shard_map/ppermute | solution.py:984
  319.2 17.3 %collective-permute-start.93 = (f32[2112,128]{1,0:T(8,128)S(1)}, f32[2112,128]{1,0:T(8,128)S(1)}, u32[]{:S(2)}, u32[]{:S(2)}) collective-permute-start(f32[2112,128]{1,0:T(8,128)S(1)} %pad_maximum_fusion.7), channel_id=1, source_target_pairs={{0,2},{1,5},{2,0},{3,7},{4,6},{5,1},{6,4},{7,3},{8,10},{9,13},{10,... | collective-permute-start | bytes 3244040 | tf_op jit(solution)/shard_map/ppermute | solution.py:984
  324.5 13.8 %collective-permute-start.95 = (f32[192,128]{1,0:T(8,128)S(1)}, f32[192,128]{1,0:T(8,128)S(1)}, u32[]{:S(2)}, u32[]{:S(2)}) collective-permute-start(f32[192,128]{1,0:T(8,128)S(1)} %bitcast.210), channel_id=1, source_target_pairs={{0,6},{1,7},{2,4},{3,5},{4,2},{5,3},{6,0},{7,1},{8,14},{9,15},{10,... | collective-permute-start | bytes 294920 | tf_op jit(solution)/shard_map/ppermute | solution.py:984
  325.9 12.4 %collective-permute-start.94 = (f32[192,128]{1,0:T(8,128)S(1)}, f32[192,128]{1,0:T(8,128)S(1)}, u32[]{:S(2)}, u32[]{:S(2)}) collective-permute-start(f32[192,128]{1,0:T(8,128)S(1)} %bitcast.211), channel_id=1, source_target_pairs={{0,4},{1,3},{2,6},{3,1},{4,0},{5,7},{6,2},{7,5},{8,12},{9,11},{10,... | collective-permute-start | bytes 294920 | tf_op jit(solution)/shard_map/ppermute | solution.py:984
  (114 other events, 811.4 us)
